TPU v7x, 128 devices: a whole 4x4x4 slice. The times are simulated.
128 devices in a mesh: tm: 2 (over core), tile: 64 (over z, y, x).
Axes of the slice: x: 4, y: 4, z: 4, core: 2. Of those that a mesh axis runs over, the one named last changes fastest.
Arguments:
- frames: bfloat16 [8, 64, 64, 32, 128], P('tm', 'tile'), may hold values from -6 to 6
- w_in: bfloat16 [3, 3, 128, 128], replicated, may hold values from -0.1875 to 0.1875
- w_out: bfloat16 [3, 3, 128, 128], replicated, may hold values from -0.1875 to 0.1875
- decay: float32 [8, 128], P('tm'), may hold values from 0 to 1
- skip: float32 [128], replicated, may hold values from 0.5 to 1.5
Outputs:
- mixed: bfloat16 [8, 64, 64, 32, 128], P('tm', 'tile')
All inputs are finite; a program needn't handle non-finite values.
Results may differ from a plain program's by a relative error of at most 0.006.
Values may be sent and summed in bfloat16 or wider, within the bound.
A program may use at most 64 MiB of HBM per device.

v0:
```python
import jax
import jax.numpy as jnp
from jax import lax
from jax.sharding import PartitionSpec as P

TROWS = 4


def passed_along(value, axis, by):
    size = lax.axis_size(axis)
    return lax.ppermute(value, axis, [(i, (i + by) % size) for i in range(size)])


def from_behind(value, axis, steps):
    count = lax.axis_size(axis)
    initial, last = (max(0, -steps), min(count, count - steps))
    return lax.ppermute(value, axis, [(source, source + steps) for source in range(initial, last)])


def side_edge(piece, by):
    return passed_along(piece, "tile", by)


def row_edge(piece, by):
    return passed_along(piece, "tile", by)


def bordered(field, column, row_index, tcols, trows):
    edges = [
        side_edge(field[:, :, -1:, :] if by == 1 else field[:, :, :1, :], by) for by in (1, -1)
    ]
    left_col = jnp.where(column > 0, edges[0], jnp.zeros_like(edges[0]))
    right_col = jnp.where(column < tcols - 1, edges[1], jnp.zeros_like(edges[1]))
    widened = jnp.concatenate([left_col, field, right_col], axis=2)
    rims = [
        row_edge(widened[:, -1:] if by == tcols else widened[:, :1], by) for by in (tcols, -tcols)
    ]
    upper_rim = jnp.where(row_index > 0, rims[0], jnp.zeros_like(rims[0]))
    lower_rim = jnp.where(row_index < trows - 1, rims[1], jnp.zeros_like(rims[1]))
    return jnp.concatenate([upper_rim, widened, lower_rim], axis=1)


def convolve(padded, weight, rows, cols):
    count = padded.shape[0]
    depth = padded.shape[3]
    total = jnp.zeros((count * rows * cols, weight.shape[3]), jnp.float32)
    for shift_row in range(3):
        for shift_col in range(3):
            window = padded[
                :, shift_row : shift_row + rows, shift_col : shift_col + cols, :
            ].reshape(-1, depth)
            total = total + jnp.dot(
                window, weight[shift_row, shift_col], preferred_element_type=jnp.float32
            )
    return total.reshape(count, rows, cols, weight.shape[3])


def per_device(frames, w_in, w_out, decay, skip):
    tile_count = lax.axis_size("tile")
    tcols = tile_count // TROWS
    tile_number = (lax.axis_index("tile") + tile_count - 1) % tile_count
    column = tile_number % tcols
    row_index = tile_number // tcols
    video = frames[:, 0]
    count, rows, cols, _ = video.shape
    drive = convolve(bordered(video, column, row_index, tcols, TROWS), w_in, rows, cols)
    state = jnp.zeros((rows, cols, w_in.shape[3]), jnp.float32)
    factor = jnp.ones((w_in.shape[3],), jnp.float32)
    local_states = []
    factors = []
    for frame in range(count):
        state = decay[frame] * state + drive[frame]
        factor = factor * decay[frame]
        local_states.append(state)
        factors.append(factor)
    incoming = from_behind(state.astype(jnp.bfloat16), "tm", 1).astype(state.dtype)
    states_bf = jnp.stack(
        [local_states[frame] + factors[frame] * incoming for frame in range(count)]
    ).astype(jnp.bfloat16)
    readout = convolve(bordered(states_bf, column, row_index, tcols, TROWS), w_out, rows, cols)
    mixed = readout + skip * video.astype(jnp.float32)
    return mixed.astype(jnp.bfloat16)[:, None]


def solution(mesh):
    return jax.shard_map(
        per_device,
        mesh=mesh,
        in_specs=(P("tm", "tile", None, None, None), P(), P(), P("tm", None), P()),
        out_specs=P("tm", "tile", None, None, None),
        check_vma=False,
    )
```

profile of v0, /device:TPU:1, one launch (start us, length us, event | category | flops | bytes accessed | tf_op | source)
XLA Modules:
  0.0 82.0 jit_solution(6578153701561833698)
XLA Ops:
  0.0 1.6 %fusion.62 = (bf16[4,64,1,128]{3,2,1,0:T(2,128)(2,1)S(1)}, bf16[4,64,1,128]{3,2,1,0:T(2,128)(2,1)S(1)}) fusion(bf16[4,64,32,128]{3,2,1,0:T(8,128)(2,1)} %bitcast.127), kind=kLoop, calls=%fused_computation.121 | loop fusion | bytes 262144 | tf_op jit(solution)/shard_map/slice | solution.py:30
  1.6 9.3 %collective-permute-start.1 = (bf16[4,64,1,128]{3,2,1,0:T(2,128)(2,1)S(1)}, bf16[4,64,1,128]{3,2,1,0:T(2,128)(2,1)S(1)}, u32[]{:S(2)}, u32[]{:S(2)}) collective-permute-start(bf16[4,64,1,128]{3,2,1,0:T(2,128)(2,1)S(1)} %get-tuple-element.42), channel_id=1, source_target_pairs={{0,63},{1,0},{2,1},{3,2},{4,3},{5,4},{6,5},{7,6},{8,7},{9,8},{10,9... | collective-permute-start | bytes 196616 | tf_op jit(solution)/shard_map/ppermute | solution.py:11
  10.9 0.8 %slice_bitcast_fusion.3 = (f32[128]{0:T(128)S(1)}, f32[128]{0:T(128)S(1)}, f32[128]{0:T(128)S(1)}, f32[128]{0:T(128)S(1)}) fusion(f32[4,128]{1,0:T(4,128)} %param.8), kind=kLoop, calls=%fused_computation.109 | loop fusion | bytes 4096 | tf_op jit(solution)/shard_map/mul | solution.py:72
  11.7 0.8 %fusion.50 = (f32[128]{0:T(128)S(1)}, f32[128]{0:T(128)S(1)}, f32[128]{0:T(128)S(1)}, f32[128]{0:T(128)S(1)}) fusion(f32[4,128]{1,0:T(4,128)} %param.8), kind=kLoop, calls=%fused_computation.111 | loop fusion | flops 512 | bytes 4096 | tf_op jit(solution)/shard_map/mul | solution.py:73
  13.2 6.9 %collective-permute-done = bf16[4,64,1,128]{3,2,1,0:T(2,128)(2,1)S(1)} collective-permute-done((bf16[4,64,1,128]{3,2,1,0:T(2,128)(2,1)S(1)}, bf16[4,64,1,128]{3,2,1,0:T(2,128)(2,1)S(1)}, u32[]{:S(2)}, u32[]{:S(2)}) %collective-permute-start) | collective-permute-done | bytes 65568 | tf_op jit(solution)/shard_map/ppermute | solution.py:11
  20.3 0.8 pad_maximum_fusion.19
  21.2 2.3 %pad_maximum_fusion.10 = (bf16[4,64,32,128]{3,2,1,0:T(8,128)(2,1)S(1)}, bf16[4,64,32,128]{3,2,1,0:T(8,128)(2,1)S(1)}) fusion(bf16[4,64,1,128]{3,2,1,0:T(2,128)(2,1)S(1)} %broadcast_select_fusion.1, bf16[4,64,32,128]{3,2,1,0:T(8,128)(2,1)S(1)} %bitcast.129, bf16[4,64,1,128]{3,2,1,0:T(2,128)(2,1)S(1)} %broadcast_select_fusion.3), kind=kLoop, calls=%fused_computation.29 | loop fusion | flops 8388608 | bytes 6422528 | tf_op jit(solution)/shard_map/concatenate | solution.py:34
  23.5 1.7 %collective-permute-start.2 = (bf16[4,1,34,128]{3,2,1,0:T(8,128)(2,1)S(1)}, bf16[4,1,34,128]{3,2,1,0:T(8,128)(2,1)S(1)}, u32[]{:S(2)}, u32[]{:S(2)}) collective-permute-start(bf16[4,1,34,128]{3,2,1,0:T(8,128)(2,1)S(1)} %get-tuple-element.34), channel_id=1, source_target_pairs={{0,16},{1,17},{2,18},{3,19},{4,20},{5,21},{6,22},{7,23},{8,24},{9,... | collective-permute-start | bytes 104456 | tf_op jit(solution)/shard_map/ppermute | solution.py:11
  25.2 2.6 %collective-permute-done.2 = bf16[4,1,34,128]{3,2,1,0:T(8,128)(2,1)S(1)} collective-permute-done((bf16[4,1,34,128]{3,2,1,0:T(8,128)(2,1)S(1)}, bf16[4,1,34,128]{3,2,1,0:T(8,128)(2,1)S(1)}, u32[]{:S(2)}, u32[]{:S(2)}) %collective-permute-start.2) | collective-permute-done | bytes 34848 | tf_op jit(solution)/shard_map/ppermute | solution.py:11
  27.8 3.2 %pad_maximum_fusion = (bf16[4,65,34,128]{3,2,1,0:T(8,128)(2,1)S(1)}, bf16[4,65,34,128]{3,2,1,0:T(8,128)(2,1)S(1)}) fusion(bf16[4,1,34,128]{3,2,1,0:T(8,128)(2,1)S(1)} %broadcast_select_fusion.5, bf16[4,64,1,128]{3,2,1,0:T(2,128)(2,1)S(1)} %broadcast_select_fusion.1, bf16[4,64,32,128]{3,2,1,0:T(8,128)(2,1)S(1)} %bitcast.130, ...), kind=kLoop, calls=%fused_computation.18 | loop fusion | flops 18104320 | bytes 6823936 | tf_op jit(solution)/shard_map/concatenate | solution.py:40
  31.0 3.0 %fusion.59 = (bf16[4,64,32,128]{3,2,1,0:T(8,128)(2,1)S(1)}, bf16[4,64,32,128]{3,2,1,0:T(8,128)(2,1)S(1)}, bf16[4,64,32,128]{3,2,1,0:T(8,128)(2,1)S(1)}, bf16[4,6...) fusion(bf16[4,65,34,128]{3,2,1,0:T(8,128)(2,1)S(1)} %get-tuple-element.3, ...), kind=kLoop, calls=%fused_computation.118 | loop fusion | bytes 25165824 | tf_op jit(solution)/shard_map/slice | solution.py:49
  34.7 0.7 convolution_add_fusion.15
  35.4 0.7 convolution_add_fusion.14
  36.9 0.7 convolution_add_fusion.12
  37.6 0.7 convolution_add_fusion.11
  38.3 0.7 convolution_add_fusion.10
  41.3 1.3 %collective-permute-start.4 = (bf16[64,32,128]{2,1,0:T(8,128)(2,1)S(1)}, bf16[64,32,128]{2,1,0:T(8,128)(2,1)S(1)}, u32[]{:S(2)}, u32[]{:S(2)}) collective-permute-start(bf16[64,32,128]{2,1,0:T(8,128)(2,1)S(1)} %get-tuple-element.8), channel_id=1, source_target_pairs={{0,64},{1,65},{2,66},{3,67},{4,68},{5,69},{6,70},{7,71},{8,72},{9,... | collective-permute-start | bytes 1572872 | tf_op jit(solution)/shard_map/ppermute | solution.py:17
  42.6 4.6 %collective-permute-done.4 = bf16[64,32,128]{2,1,0:T(8,128)(2,1)S(1)} collective-permute-done((bf16[64,32,128]{2,1,0:T(8,128)(2,1)S(1)}, bf16[64,32,128]{2,1,0:T(8,128)(2,1)S(1)}, u32[]{:S(2)}, u32[]{:S(2)}) %collective-permute-start.4) | collective-permute-done | bytes 524320 | tf_op jit(solution)/shard_map/ppermute | solution.py:17
  48.3 1.5 %collective-permute-start.5 = (bf16[4,64,1,128]{3,2,1,0:T(2,128)(2,1)S(1)}, bf16[4,64,1,128]{3,2,1,0:T(2,128)(2,1)S(1)}, u32[]{:S(2)}, u32[]{:S(2)}) collective-permute-start(bf16[4,64,1,128]{3,2,1,0:T(2,128)(2,1)S(1)} %get-tuple-element.37), channel_id=1, source_target_pairs={{0,1},{1,2},{2,3},{3,4},{4,5},{5,6},{6,7},{7,8},{8,9},{9,10},{10,1... | collective-permute-start | bytes 196616 | tf_op jit(solution)/shard_map/ppermute | solution.py:11
  49.8 3.5 %collective-permute-done.6 = bf16[4,64,1,128]{3,2,1,0:T(2,128)(2,1)S(1)} collective-permute-done((bf16[4,64,1,128]{3,2,1,0:T(2,128)(2,1)S(1)}, bf16[4,64,1,128]{3,2,1,0:T(2,128)(2,1)S(1)}, u32[]{:S(2)}, u32[]{:S(2)}) %collective-permute-start.6) | collective-permute-done | bytes 65568 | tf_op jit(solution)/shard_map/ppermute | solution.py:11
  53.4 5.4 %collective-permute-done.5 = bf16[4,64,1,128]{3,2,1,0:T(2,128)(2,1)S(1)} collective-permute-done((bf16[4,64,1,128]{3,2,1,0:T(2,128)(2,1)S(1)}, bf16[4,64,1,128]{3,2,1,0:T(2,128)(2,1)S(1)}, u32[]{:S(2)}, u32[]{:S(2)}) %collective-permute-start.5) | collective-permute-done | bytes 65568 | tf_op jit(solution)/shard_map/ppermute | solution.py:11
  59.3 2.8 %pad_maximum_fusion.2 = (bf16[4,64,32,128]{3,2,1,0:T(8,128)(2,1)S(1)}, bf16[4,64,32,128]{3,2,1,0:T(8,128)(2,1)S(1)}) fusion(bf16[4,64,1,128]{3,2,1,0:T(2,128)(2,1)S(1)} %broadcast_select_fusion, bf16[1,64,32,128]{3,2,1,0:T(8,128)(2,1)S(1)} %get-tuple-element.46, bf16[1,64,32,128]{3,2,1,0:T(8,128)(2,1)S(1)} %get-tuple-element.44, ...), kind=kLoop, calls=%fused_computation.21 | loop fusion | flops 20971520 | bytes 6422528 | tf_op jit(solution)/shard_map/concatenate | solution.py:34
  62.1 1.5 %collective-permute-start.7 = (bf16[4,1,34,128]{3,2,1,0:T(8,128)(2,1)S(1)}, bf16[4,1,34,128]{3,2,1,0:T(8,128)(2,1)S(1)}, u32[]{:S(2)}, u32[]{:S(2)}) collective-permute-start(bf16[4,1,34,128]{3,2,1,0:T(8,128)(2,1)S(1)} %get-tuple-element.30), channel_id=1, source_target_pairs={{0,16},{1,17},{2,18},{3,19},{4,20},{5,21},{6,22},{7,23},{8,24},{9,... | collective-permute-start | bytes 104456 | tf_op jit(solution)/shard_map/ppermute | solution.py:11
  63.6 2.6 %collective-permute-done.7 = bf16[4,1,34,128]{3,2,1,0:T(8,128)(2,1)S(1)} collective-permute-done((bf16[4,1,34,128]{3,2,1,0:T(8,128)(2,1)S(1)}, bf16[4,1,34,128]{3,2,1,0:T(8,128)(2,1)S(1)}, u32[]{:S(2)}, u32[]{:S(2)}) %collective-permute-start.7) | collective-permute-done | bytes 34848 | tf_op jit(solution)/shard_map/ppermute | solution.py:11
  66.2 4.4 %pad_maximum_fusion.1 = (bf16[4,65,34,128]{3,2,1,0:T(8,128)(2,1)S(1)}, bf16[4,65,34,128]{3,2,1,0:T(8,128)(2,1)S(1)}) fusion(bf16[4,1,34,128]{3,2,1,0:T(8,128)(2,1)S(1)} %broadcast_select_fusion.4, bf16[4,64,1,128]{3,2,1,0:T(2,128)(2,1)S(1)} %broadcast_select_fusion, bf16[1,64,32,128]{3,2,1,0:T(8,128)(2,1)S(1)} %get-tuple-element.46, ...), kind=kLoop, calls=%fused_computation.20 | loop fusion | flops 31682560 | bytes 6823936 | tf_op jit(solution)/shard_map/concatenate | solution.py:40
  70.7 1.5 %fusion.58 = (bf16[4,64,32,128]{3,2,1,0:T(8,128)(2,1)S(1)}, bf16[4,64,32,128]{3,2,1,0:T(8,128)(2,1)S(1)}, bf16[4,64,32,128]{3,2,1,0:T(8,128)(2,1)S(1)}) fusion(bf16[4,65,34,128]{3,2,1,0:T(8,128)(2,1)S(1)} %get-tuple-element.28), kind=kLoop, calls=%fused_computation.117 | loop fusion | bytes 12582912 | tf_op jit(solution)/shard_map/slice | solution.py:49
  72.1 1.3 %fusion.57 = (bf16[4,64,32,128]{3,2,1,0:T(8,128)(2,1)S(1)}, bf16[4,64,32,128]{3,2,1,0:T(8,128)(2,1)S(1)}, bf16[4,64,32,128]{3,2,1,0:T(8,128)(2,1)S(1)}) fusion(bf16[4,65,34,128]{3,2,1,0:T(8,128)(2,1)S(1)} %get-tuple-element.27), kind=kLoop, calls=%fused_computation.116 | loop fusion | bytes 12582912 | tf_op jit(solution)/shard_map/slice | solution.py:49
  74.1 0.7 convolution_add_fusion.7
  75.6 0.7 convolution_add_fusion.5
  76.3 0.7 convolution_add_fusion.4
  77.7 0.7 convolution_add_fusion.2
  79.9 2.1 %add_convert_fusion = bf16[4,1,64,32,128]{4,3,2,1,0:T(8,128)(2,1)} fusion(f32[4,1,64,32,128]{4,3,2,1,0:T(8,128)S(1)} %bitcast.132, bf16[4,1,64,32,128]{4,3,2,1,0:T(8,128)(2,1)S(1)} %copy-done, f32[128]{0:T(128)S(1)} %copy-done.3), kind=kLoop, calls=%fused_computation.16 | loop fusion | flops 4194304 | bytes 8389120 | tf_op jit(solution)/shard_map/convert_element_type | solution.py:82
  (38 shorter events, 9.8 us)
Async XLA Ops:
  0.0 21.2 %copy-start = (bf16[4,1,64,32,128]{4,3,2,1,0:T(8,128)(2,1)S(1)}, bf16[4,1,64,32,128]{4,3,2,1,0:T(8,128)(2,1)}, u32[]{:S(2)}) copy-start(bf16[4,1,64,32,128]{4,3,2,1,0:T(8,128)(2,1)} %param.5) | copy-start | bytes 6291460
  1.6 11.5 %collective-permute-start.1 = (bf16[4,64,1,128]{3,2,1,0:T(2,128)(2,1)S(1)}, bf16[4,64,1,128]{3,2,1,0:T(2,128)(2,1)S(1)}, u32[]{:S(2)}, u32[]{:S(2)}) collective-permute-start(bf16[4,64,1,128]{3,2,1,0:T(2,128)(2,1)S(1)} %get-tuple-element.42), channel_id=1, source_target_pairs={{0,63},{1,0},{2,1},{3,2},{4,3},{5,4},{6,5},{7,6},{8,7},{9,8},{10,9... | collective-permute-start | bytes 196616 | tf_op jit(solution)/shard_map/ppermute | solution.py:11
  10.9 9.2 %collective-permute-start = (bf16[4,64,1,128]{3,2,1,0:T(2,128)(2,1)S(1)}, bf16[4,64,1,128]{3,2,1,0:T(2,128)(2,1)S(1)}, u32[]{:S(2)}, u32[]{:S(2)}) collective-permute-start(bf16[4,64,1,128]{3,2,1,0:T(2,128)(2,1)S(1)} %get-tuple-element.41), channel_id=1, source_target_pairs={{0,1},{1,2},{2,3},{3,4},{4,5},{5,6},{6,7},{7,8},{8,9},{9,10},{10,1... | collective-permute-start | bytes 196616 | tf_op jit(solution)/shard_map/ppermute | solution.py:11
  21.1 4.1 %collective-permute-start.3 = (bf16[4,1,34,128]{3,2,1,0:T(8,128)(2,1)S(1)}, bf16[4,1,34,128]{3,2,1,0:T(8,128)(2,1)S(1)}, u32[]{:S(2)}, u32[]{:S(2)}) collective-permute-start(bf16[4,1,34,128]{3,2,1,0:T(8,128)(2,1)S(1)} %get-tuple-element.33), channel_id=1, source_target_pairs={{0,48},{1,49},{2,50},{3,51},{4,52},{5,53},{6,54},{7,55},{8,56},{9,... | collective-permute-start | bytes 104456 | tf_op jit(solution)/shard_map/ppermute | solution.py:11
  23.5 4.3 %collective-permute-start.2 = (bf16[4,1,34,128]{3,2,1,0:T(8,128)(2,1)S(1)}, bf16[4,1,34,128]{3,2,1,0:T(8,128)(2,1)S(1)}, u32[]{:S(2)}, u32[]{:S(2)}) collective-permute-start(bf16[4,1,34,128]{3,2,1,0:T(8,128)(2,1)S(1)} %get-tuple-element.34), channel_id=1, source_target_pairs={{0,16},{1,17},{2,18},{3,19},{4,20},{5,21},{6,22},{7,23},{8,24},{9,... | collective-permute-start | bytes 104456 | tf_op jit(solution)/shard_map/ppermute | solution.py:11
  31.0 3.0 %copy-start.1 = (bf16[3,3,128,128]{3,2,1,0:T(8,128)(2,1)S(1)}, bf16[3,3,128,128]{3,2,1,0:T(8,128)(2,1)}, u32[]{:S(2)}) copy-start(bf16[3,3,128,128]{3,2,1,0:T(8,128)(2,1)} %param.6) | copy-start | bytes 884740
  41.3 5.9 %collective-permute-start.4 = (bf16[64,32,128]{2,1,0:T(8,128)(2,1)S(1)}, bf16[64,32,128]{2,1,0:T(8,128)(2,1)S(1)}, u32[]{:S(2)}, u32[]{:S(2)}) collective-permute-start(bf16[64,32,128]{2,1,0:T(8,128)(2,1)S(1)} %get-tuple-element.8), channel_id=1, source_target_pairs={{0,64},{1,65},{2,66},{3,67},{4,68},{5,69},{6,70},{7,71},{8,72},{9,... | collective-permute-start | bytes 1572872 | tf_op jit(solution)/shard_map/ppermute | solution.py:17
  48.2 5.0 %collective-permute-start.6 = (bf16[4,64,1,128]{3,2,1,0:T(2,128)(2,1)S(1)}, bf16[4,64,1,128]{3,2,1,0:T(2,128)(2,1)S(1)}, u32[]{:S(2)}, u32[]{:S(2)}) collective-permute-start(bf16[4,64,1,128]{3,2,1,0:T(2,128)(2,1)S(1)} %get-tuple-element.38), channel_id=1, source_target_pairs={{0,63},{1,0},{2,1},{3,2},{4,3},{5,4},{6,5},{7,6},{8,7},{9,8},{10,9... | collective-permute-start | bytes 196616 | tf_op jit(solution)/shard_map/ppermute | solution.py:11
  48.3 10.4 %collective-permute-start.5 = (bf16[4,64,1,128]{3,2,1,0:T(2,128)(2,1)S(1)}, bf16[4,64,1,128]{3,2,1,0:T(2,128)(2,1)S(1)}, u32[]{:S(2)}, u32[]{:S(2)}) collective-permute-start(bf16[4,64,1,128]{3,2,1,0:T(2,128)(2,1)S(1)} %get-tuple-element.37), channel_id=1, source_target_pairs={{0,1},{1,2},{2,3},{3,4},{4,5},{5,6},{6,7},{7,8},{8,9},{9,10},{10,1... | collective-permute-start | bytes 196616 | tf_op jit(solution)/shard_map/ppermute | solution.py:11
  59.0 4.6 %collective-permute-start.8 = (bf16[4,1,34,128]{3,2,1,0:T(8,128)(2,1)S(1)}, bf16[4,1,34,128]{3,2,1,0:T(8,128)(2,1)S(1)}, u32[]{:S(2)}, u32[]{:S(2)}) collective-permute-start(bf16[4,1,34,128]{3,2,1,0:T(8,128)(2,1)S(1)} %get-tuple-element.29), channel_id=1, source_target_pairs={{0,48},{1,49},{2,50},{3,51},{4,52},{5,53},{6,54},{7,55},{8,56},{9,... | collective-permute-start | bytes 104456 | tf_op jit(solution)/shard_map/ppermute | solution.py:11
  62.1 4.1 %collective-permute-start.7 = (bf16[4,1,34,128]{3,2,1,0:T(8,128)(2,1)S(1)}, bf16[4,1,34,128]{3,2,1,0:T(8,128)(2,1)S(1)}, u32[]{:S(2)}, u32[]{:S(2)}) collective-permute-start(bf16[4,1,34,128]{3,2,1,0:T(8,128)(2,1)S(1)} %get-tuple-element.30), channel_id=1, source_target_pairs={{0,16},{1,17},{2,18},{3,19},{4,20},{5,21},{6,22},{7,23},{8,24},{9,... | collective-permute-start | bytes 104456 | tf_op jit(solution)/shard_map/ppermute | solution.py:11
  72.1 1.3 %copy-start.2 = (bf16[3,3,128,128]{3,2,1,0:T(8,128)(2,1)S(1)}, bf16[3,3,128,128]{3,2,1,0:T(8,128)(2,1)}, u32[]{:S(2)}) copy-start(bf16[3,3,128,128]{3,2,1,0:T(8,128)(2,1)} %param.7) | copy-start | bytes 884740
  79.2 0.7 copy-start.3
where the time goes:
time: 82.9 us; the launch traced here: 82 us
  waiting for transfers between devices  26.1 us (31%)
  other arithmetic  18.5 us (22%)
  starting transfers between devices  15.7 us (19%)
  matrix products  12.7 us (15%)
  local copies, waits for them, and re-layouts  8.67 us (10%)
    ppermute x8, waiting for transfers between devices, passed_along(): lax.ppermute(value, axis, [(i, (i + by) % size) for i in range(size)])  21.5 us
    ppermute x8, starting transfers between devices, passed_along(): lax.ppermute(value, axis, [(i, (i + by) % size) for i in range(size)])  14.4 us
    dot_general x18, matrix products, convolve(): jnp.dot(window, weight[shift_row, shift_col], preferred_element_type=jnp....  12.7 us
    concatenate x2, other arithmetic, bordered(): return jnp.concatenate([upper_rim, widened, lower_rim], axis=1)  7.59 us
    concatenate x4, other arithmetic, bordered(): widened = jnp.concatenate([left_col, field, right_col], axis=2)  5.97 us
    slice x3, local copies, waits for them, and re-layouts, convolve(): padded[:, shift_row:shift_row + rows, shift_col:shift_col + cols, :]  5.76 us
    ppermute x1, waiting for transfers between devices, from_behind(): lax.ppermute(value, axis, [(source, source + steps) for source in range(i...  4.61 us
    convert_element_type x1, other arithmetic, per_device(): return mixed.astype(jnp.bfloat16)[:, None]  2.12 us
  transfers between devices with their start and end apart: 9, of which 7 were waited for; matrix products, arithmetic and copies ran while one was open for 9% of the time, Pallas kernels for 0%

commit v1 on v0

v1 whole, which is shorter than its diff:
```python
import functools

import jax
import jax.numpy as jnp
from jax import lax
from jax.experimental import pallas as pl
from jax.experimental.pallas import tpu as pltpu
from jax.sharding import PartitionSpec as P

TROWS = 4
C = 128
BF = jnp.bfloat16
F32 = jnp.float32
MESH = pl.DeviceIdType.MESH

TOP = 16


def mm(lhs, rhs):
    return jnp.dot(lhs, rhs, preferred_element_type=F32)


def pair_weights(w, pair):
    zero = jnp.zeros((C, C), BF)
    for i in range(4):
        for b in range(3):
            rows = pl.ds((i * 3 + b) * C, C)
            pair[rows, 0:C] = w[i, b] if i < 3 else zero
            pair[rows, C : 2 * C] = w[i - 1, b] if i > 0 else zero


def side_weights(w, side):
    zero = jnp.zeros((C, C), BF)
    for s in range(2):
        ring = (1, 0, 2) if s == 0 else (1, 2, 0)
        edge = 0 if s == 0 else 2
        for a in range(3):
            for k in range(3):
                rows = pl.ds(k * C, C)
                side[s, rows, a * 2 * C : a * 2 * C + C] = w[a, ring[k]]
                side[s, rows, a * 2 * C + C : (a + 1) * 2 * C] = w[a, edge] if k == 0 else zero


def pair_rows(block, pairs):
    cols, depth = block.shape[1:]
    split = block.reshape(pairs + 1, 2, cols, depth)
    even, odd = split[:, 0], split[:, 1]
    taps = [even[:pairs], odd[:pairs], even[1:], odd[1:]]
    return jnp.concatenate(taps, axis=-1).reshape(pairs * cols, 4 * depth)


def kernel(
    trows, frames, w_in, w_out, decay, skip, out,
    x, x3, s3, loc, w1, w2, pw1, pw2, sw, edge, z, y, ss, stage, lo, inc, so, si, o,
    load_sem, w_sem, send_sem, recv_sem, tsend_sem, trecv_sem, out_sem,
):
    count, rows, cols, _ = frames.shape
    tiles = lax.axis_size("tile")
    tcols = tiles // trows
    me = lax.axis_index("tile")
    tm = lax.axis_index("tm")
    k = lax.rem(me + tiles - 1, tiles)
    column = lax.rem(k, tcols)
    row_index = k // tcols

    loads = [
        pltpu.make_async_copy(frames.at[f], x.at[f, pl.ds(2, rows)], load_sem.at[f])
        for f in range(count)
    ]
    for c in loads:
        c.start()
    wloads = [
        pltpu.make_async_copy(w_in, w1, w_sem.at[0]),
        pltpu.make_async_copy(w_out, w2, w_sem.at[1]),
    ]
    for c in wloads:
        c.start()

    def at(by):
        return lax.rem(me + by + tiles, tiles)

    barrier = pltpu.get_barrier_semaphore()
    steps = (-1, 1, -tcols, tcols, -tcols - 1, -tcols + 1, tcols - 1, tcols + 1)
    for by in steps:
        pl.semaphore_signal(barrier, inc=1, device_id=(tm, at(by)), device_id_type=MESH)
    pl.semaphore_signal(barrier, inc=1, device_id=(1 - tm, me), device_id_type=MESH)

    for f in range(count):
        loads[f].wait()
        first = x[f, 2 : 2 + rows, 0:16, :].astype(F32)[:, 0:8, :]
        stage[0] = first.reshape(rows * 8, C)
        last = x[f, 2 : 2 + rows, cols - 16 : cols, :].astype(F32)[:, 8:16, :]
        stage[1] = last.reshape(rows * 8, C)
        for s in range(2):
            for n in range(2):
                offset = n if s == 0 else 7 - n
                value = stage[s, pl.ds(offset, rows, stride=8), :].astype(BF)
                edge[s, n, f] = value
                if n == 0:
                    z[s, 2, f, TOP : TOP + rows] = value

    pl.semaphore_wait(barrier, 9)

    low, mid, high = pl.ds(0, TOP), pl.ds(TOP, rows), pl.ds(TOP + rows, TOP)
    head, tail = pl.ds(0, TOP), pl.ds(rows - TOP, TOP)
    two = pl.ds(0, 2)
    plan = [
        (edge.at[0], z.at[1, two, :, mid], -1),
        (edge.at[1], z.at[0, two, :, mid], 1),
        (frames.at[:, pl.ds(0, 2)], x.at[:, pl.ds(rows + 2, 2)], -tcols),
        (frames.at[:, pl.ds(rows - 2, 2)], x.at[:, pl.ds(0, 2)], tcols),
        (edge.at[:, 0, :, head], z.at[:, 2, :, high], -tcols),
        (edge.at[:, 0, :, tail], z.at[:, 2, :, low], tcols),
        (edge.at[0, :, :, head], z.at[1, two, :, high], -tcols - 1),
        (edge.at[1, :, :, head], z.at[0, two, :, high], -tcols + 1),
        (edge.at[0, :, :, tail], z.at[1, two, :, low], tcols - 1),
        (edge.at[1, :, :, tail], z.at[0, two, :, low], tcols + 1),
    ]
    sends = [
        pltpu.make_async_remote_copy(
            src_ref=src, dst_ref=dst, send_sem=send_sem.at[i], recv_sem=recv_sem.at[i],
            device_id=(tm, at(by)), device_id_type=MESH,
        )
        for i, (src, dst, by) in enumerate(plan)
    ]
    for c in sends:
        c.start()

    wloads[0].wait()
    pair_weights(w1, pw1)
    side_weights(w1, sw)

    column_of = lax.broadcasted_iota(jnp.int32, (1, cols, C), 1)

    def widen(f, start, size):
        block = x[f, pl.ds(start, size)]
        wide = block.astype(F32)
        left = jnp.where(column_of == 0, 0.0, pltpu.roll(wide, 1, 1))
        right = jnp.where(column_of == cols - 1, 0.0, pltpu.roll(wide, cols - 1, 1))
        x3[f, pl.ds(start, size), :, 0:C] = left.astype(BF)
        x3[f, pl.ds(start, size), :, C : 2 * C] = block
        x3[f, pl.ds(start, size), :, 2 * C : 3 * C] = right.astype(BF)

    for f in range(count):
        @pl.loop(0, rows // 8)
        def _(i):
            widen(f, 2 + i * 8, 8)

    def exchange(i, src, dst):
        return pltpu.make_async_remote_copy(
            src_ref=src, dst_ref=dst, send_sem=tsend_sem.at[i], recv_sem=trecv_sem.at[i],
            device_id=(1 - tm, me), device_id_type=MESH,
        )

    half = rows // 4
    chunks = [(1, half), (1 + half, rows // 2 - 1 - half)]
    hands = [
        exchange(0, lo.at[pl.ds(*chunks[0])], inc.at[pl.ds(*chunks[0])]),
        exchange(1, lo.at[pl.ds(*chunks[1])], inc.at[pl.ds(*chunks[1])]),
        exchange(2, lo.at[pl.ds(0, 1)], inc.at[pl.ds(0, 1)]),
        exchange(3, lo.at[pl.ds(rows // 2, 1)], inc.at[pl.ds(rows // 2, 1)]),
        exchange(4, so, si),
    ]

    def recur(f, q, size, drive):
        drive = drive.reshape(size, cols, 2 * C)
        for e in range(2):
            value = drive[:, :, e * C : (e + 1) * C]
            if f > 0:
                value = decay[f : f + 1, :] * loc[f - 1, pl.ds(q, size), e] + value
            loc[f, pl.ds(q, size), e] = value
            if f == count - 1:
                lo[pl.ds(q, size), e] = value.astype(BF)

    for n, (q, size) in enumerate(chunks):
        for f in range(count):
            lhs = pair_rows(x3[f, 2 * q : 2 * q + 2 * size + 2], size)
            recur(f, q, size, mm(lhs, pw1[...]))

        @pl.when(tm == 0)
        def _():
            hands[n].start()

    for c in sends:
        c.wait_recv()
    for f in range(count):
        widen(f, 0, 2)
        widen(f, rows + 2, 2)

    @pl.when(row_index == 0)
    def _():
        x3[:, 0:2] = jnp.zeros((count, 2, cols, 3 * C), BF)

    @pl.when(row_index == trows - 1)
    def _():
        x3[:, rows + 2 : rows + 4] = jnp.zeros((count, 2, cols, 3 * C), BF)

    for q in (0, rows // 2):
        lhs = jnp.concatenate([pair_rows(x3[f, 2 * q : 2 * q + 4], 1) for f in range(count)], axis=0)
        drive = mm(lhs, pw1[...])
        for f in range(count):
            recur(f, q, 1, drive[f * cols : (f + 1) * cols])

    @pl.when(tm == 0)
    def _():
        hands[2].start()
        hands[3].start()

    span = rows + 2 * TOP
    for s in range(2):
        lhs = jnp.concatenate([z[s, n].reshape(count * span, C) for n in range(3)], axis=-1)
        result = mm(lhs, sw[s])
        for a in range(3):
            y[s, a] = result[:, a * 2 * C : (a + 1) * 2 * C].reshape(count, span, 2 * C)

    @pl.when(row_index == 0)
    def _():
        y[:, :, :, 0:TOP] = jnp.zeros((2, 3, count, TOP, 2 * C), F32)

    @pl.when(row_index == trows - 1)
    def _():
        y[:, :, :, TOP + rows : span] = jnp.zeros((2, 3, count, TOP, 2 * C), F32)

    tall = rows + 16
    for s in range(2):
        inside = jnp.where(column > 0 if s == 0 else column < tcols - 1, 1.0, 0.0).astype(F32)
        for e in range(2):
            lanes = slice(e * C, (e + 1) * C)
            state = None
            for f in range(count):
                drive = (
                    y[s, 0, f, 7 : 7 + tall, lanes] + y[s, 1, f, 8 : 8 + tall, lanes] + y[s, 2, f, 9 : 9 + tall, lanes]
                ) * inside
                state = drive if f == 0 else decay[f : f + 1, :] * state + drive
                ss[s, e, f] = state
            so[s, e] = state.astype(BF)

    @pl.when(tm == 0)
    def _():
        hands[4].start()
        inc[...] = jnp.zeros(inc.shape, BF)
        si[...] = jnp.zeros(si.shape, BF)

    wloads[1].wait()
    pair_weights(w2, pw2)

    @pl.when(tm == 1)
    def _():
        for c in hands:
            c.wait_recv()

    factors = []
    for f in range(count):
        keep = decay[f : f + 1, :]
        factors.append(keep if f == 0 else factors[-1] * keep)
    for s in range(2):
        for e in range(2):
            arrived = si[s, e].astype(F32)
            for f in range(count):
                ss[s, e, f] = ss[s, e, f] + factors[f] * arrived

    column_in = lax.broadcasted_iota(jnp.int32, (cols, C), 0)

    @pl.loop(0, rows // 2 + 1)
    def _(q):
        for e in range(2):
            arrived = inc[q, e].astype(F32)
            at_row = 2 * q + e
            side = pl.ds(at_row + 7, 1)
            for f in range(count):
                state = loc[f, q, e] + factors[f] * arrived
                state = state + jnp.where(column_in == 0, ss[0, 1, f, side, :], 0.0)
                state = state + jnp.where(column_in == cols - 1, ss[1, 1, f, side, :], 0.0)
                left = jnp.where(column_in == 0, ss[0, 0, f, side, :], pltpu.roll(state, 1, 0))
                right = jnp.where(column_in == cols - 1, ss[1, 0, f, side, :], pltpu.roll(state, cols - 1, 0))
                s3[f, at_row, :, 0:C] = left.astype(BF)
                s3[f, at_row, :, C : 2 * C] = state.astype(BF)
                s3[f, at_row, :, 2 * C : 3 * C] = right.astype(BF)

    @pl.when(row_index == 0)
    def _():
        s3[:, 0:1] = jnp.zeros((count, 1, cols, 3 * C), BF)

    @pl.when(row_index == trows - 1)
    def _():
        s3[:, rows + 1 : rows + 2] = jnp.zeros((count, 1, cols, 3 * C), BF)

    stores = []
    for f in range(count):
        for n in range(2):
            lhs = pair_rows(s3[f, 2 * n * half : 2 * (n + 1) * half + 2], half)
            result = mm(lhs, pw2[...]).reshape(half, cols, 2 * C)
            base = 2 * n * half
            video = x[f, 2 + base : 2 + base + 2 * half].astype(F32).reshape(half, 2, cols, C)
            for e in range(2):
                mixed = result[:, :, e * C : (e + 1) * C] + skip[...] * video[:, e]
                o[f, n * half : (n + 1) * half, e] = mixed.astype(BF)
            store = pltpu.make_async_copy(
                o.at[f, pl.ds(n * half, half)], out.at[f, pl.ds(n * half, half)], out_sem.at[2 * f + n]
            )
            store.start()
            stores.append(store)

    for c in sends:
        c.wait_send()

    @pl.when(tm == 0)
    def _():
        for c in hands:
            c.wait_send()

    for c in stores:
        c.wait()


def per_device(frames, w_in, w_out, decay, skip):
    count, _, rows, cols, _ = frames.shape
    pairs = rows // 2 + 1
    span = rows + 2 * TOP
    tall = rows + 16
    anywhere = pl.BlockSpec(memory_space=pl.ANY)
    vmem = pl.BlockSpec(memory_space=pltpu.VMEM)
    out = pl.pallas_call(
        functools.partial(kernel, TROWS),
        out_shape=jax.ShapeDtypeStruct((count, rows // 2, 2, cols, C), BF),
        in_specs=[anywhere, anywhere, anywhere, vmem, vmem],
        out_specs=anywhere,
        scratch_shapes=[
            pltpu.VMEM((count, rows + 4, cols, C), BF),
            pltpu.VMEM((count, rows + 4, cols, 3 * C), BF),
            pltpu.VMEM((count, rows + 2, cols, 3 * C), BF),
            pltpu.VMEM((count, pairs, 2, cols, C), F32),
            pltpu.VMEM((3, 3, C, C), BF),
            pltpu.VMEM((3, 3, C, C), BF),
            pltpu.VMEM((12 * C, 2 * C), BF),
            pltpu.VMEM((12 * C, 2 * C), BF),
            pltpu.VMEM((2, 3 * C, 6 * C), BF),
            pltpu.VMEM((2, 2, count, rows, C), BF),
            pltpu.VMEM((2, 3, count, span, C), BF),
            pltpu.VMEM((2, 3, count, span, 2 * C), F32),
            pltpu.VMEM((2, 2, count, tall, C), F32),
            pltpu.VMEM((2, rows * 8, C), F32),
            pltpu.VMEM((pairs, 2, cols, C), BF),
            pltpu.VMEM((pairs, 2, cols, C), BF),
            pltpu.VMEM((2, 2, tall, C), BF),
            pltpu.VMEM((2, 2, tall, C), BF),
            pltpu.VMEM((count, rows // 2, 2, cols, C), BF),
            pltpu.SemaphoreType.DMA((count,)),
            pltpu.SemaphoreType.DMA((2,)),
            pltpu.SemaphoreType.DMA((10,)),
            pltpu.SemaphoreType.DMA((10,)),
            pltpu.SemaphoreType.DMA((5,)),
            pltpu.SemaphoreType.DMA((5,)),
            pltpu.SemaphoreType.DMA((2 * count,)),
        ],
        compiler_params=pltpu.CompilerParams(
            collective_id=0, has_side_effects=True, vmem_limit_bytes=56 * 2**20
        ),
    )(frames[:, 0], w_in, w_out, decay, skip.reshape(1, C))
    return out.reshape(count, 1, rows, cols, C)


def solution(mesh):
    return jax.shard_map(
        per_device,
        mesh=mesh,
        in_specs=(P("tm", "tile", None, None, None), P(), P(), P("tm", None), P()),
        out_specs=P("tm", "tile", None, None, None),
        check_vma=False,
    )
```

time: 82.9 us -> 30.7 us (0.37)
  Pallas kernels: 0 us -> 27.1 us
  waiting for transfers between devices: 26.1 us -> 0 us
  other arithmetic: 18.5 us -> 0 us
  starting transfers between devices: 15.7 us -> 0 us
  matrix products: 12.7 us -> 0 us
  local copies, waits for them, and re-layouts: 8.67 us -> 3.35 us
    pallas_call x0 -> x1, Pallas kernels: none -> 27.1 us  [per_device(): pl.pallas_call(functools.partial(kernel, TROWS), out_shape=jax.ShapeDtype...]
    ppermute x9 -> x0, waiting for transfers between devices: 26.1 us -> none  [the longest x8 21.5 us: passed_along(): lax.ppermute(value, axis, [(i, (i + by) % size) for i in range(size)])]
    ppermute x9 -> x0, starting transfers between devices: 15.7 us -> none  [the longest x8 14.4 us: passed_along(): lax.ppermute(value, axis, [(i, (i + by) % size) for i in range(size)])]
    concatenate x6 -> x0, other arithmetic: 13.6 us -> none  [the longest x2 7.59 us: bordered(): return jnp.concatenate([upper_rim, widened, lower_rim], axis=1)]
    dot_general x18 -> x0, matrix products: 12.7 us -> none  [convolve(): jnp.dot(window, weight[shift_row, shift_col], preferred_element_type=jnp....]
    slice x6 -> x0, local copies, waits for them, and re-layouts: 7.81 us -> none  [the longest x3 5.76 us: convolve(): padded[:, shift_row:shift_row + rows, shift_col:shift_col + cols, :]]
    unnamed x8 -> x1, local copies, waits for them, and re-layouts: 0.02 us -> 3.35 us
    convert_element_type x2 -> x0, other arithmetic: 2.65 us -> none  [the longest x1 2.12 us: per_device(): return mixed.astype(jnp.bfloat16)[:, None]]
  transfers between devices with their start and end apart: 9 -> 0, of which waited for: 7 -> 0; matrix products, arithmetic and copies ran while one was open for 9% -> 0% of each run, Pallas kernels for 0% -> 0%
where the time goes in v1:
time: 30.7 us; the launch traced here: 30.5 us
  Pallas kernels  27.1 us (88%)
  local copies, waits for them, and re-layouts  3.35 us (11%)
    pallas_call x1, Pallas kernels, per_device(): pl.pallas_call(functools.partial(kernel, TROWS), out_shape=jax.ShapeDtype...  27.1 us
    unnamed x1, local copies, waits for them, and re-layouts  3.35 us

profile of v1, /device:TPU:1, one launch (start us, length us, event | category | flops | bytes accessed | tf_op | source)
XLA Modules:
  0.0 30.5 jit_solution(10755060800162407920)
XLA Ops:
  0.0 27.1 %shard_map.55 = bf16[4,32,2,32,128]{4,3,2,1,0:T(8,128)(2,1)} custom-call(bf16[4,64,32,128]{3,2,1,0:T(8,128)(2,1)} %bitcast.6, bf16[3,3,128,128]{3,2,1,0:T(8,128)(2,1)} %w_in.1, bf16[3,3,128,128]{3,2,1,0:T(8,128)(2,1)} %w_out.1, f32[4,128]{1,0:T(4,128)} %decay.1, f32[1,128]{1,0:T(1,128)} %bitcast.7), custom_call_target="tpu_custom_call" | custom-call | tf_op jit(solution)/shard_map/pallas_call | solution.py:323
  27.1 3.4 %copy.8 = bf16[4,1,64,32,128]{4,3,2,1,0:T(8,128)(2,1)} copy(bf16[4,1,64,32,128]{4,3,2,1,0:T(8,128)(2,1)} %bitcast.5) | data formatting | bytes 4194304

commit v2 on v1

--- a/solution.py
+++ b/solution.py
@@ -50,9 +50,9 @@
 
 
 def kernel(
-    trows, frames, w_in, w_out, decay, skip, out,
-    x, x3, s3, loc, w1, w2, pw1, pw2, sw, edge, z, y, ss, stage, lo, inc, so, si, o,
-    load_sem, w_sem, send_sem, recv_sem, tsend_sem, trecv_sem, out_sem,
+    trows, frames, w_in, w_out, decay_in, skip_in, o,
+    x, x3, s3, loc, w1, w2, pw1, pw2, sw, edge, z, y, ss, stage, lo, inc, so, si, decay, skip,
+    load_sem, w_sem, send_sem, recv_sem, tsend_sem, trecv_sem,
 ):
     count, rows, cols, _ = frames.shape
     tiles = lax.axis_size("tile")
@@ -72,6 +72,8 @@
     wloads = [
         pltpu.make_async_copy(w_in, w1, w_sem.at[0]),
         pltpu.make_async_copy(w_out, w2, w_sem.at[1]),
+        pltpu.make_async_copy(decay_in, decay, w_sem.at[2]),
+        pltpu.make_async_copy(skip_in, skip, w_sem.at[3]),
     ]
     for c in wloads:
         c.start()
@@ -127,6 +129,8 @@
         c.start()
 
     wloads[0].wait()
+    wloads[2].wait()
+    wloads[3].wait()
     pair_weights(w1, pw1)
     side_weights(w1, sw)
 
@@ -285,7 +289,6 @@
     def _():
         s3[:, rows + 1 : rows + 2] = jnp.zeros((count, 1, cols, 3 * C), BF)
 
-    stores = []
     for f in range(count):
         for n in range(2):
             lhs = pair_rows(s3[f, 2 * n * half : 2 * (n + 1) * half + 2], half)
@@ -295,11 +298,6 @@
             for e in range(2):
                 mixed = result[:, :, e * C : (e + 1) * C] + skip[...] * video[:, e]
                 o[f, n * half : (n + 1) * half, e] = mixed.astype(BF)
-            store = pltpu.make_async_copy(
-                o.at[f, pl.ds(n * half, half)], out.at[f, pl.ds(n * half, half)], out_sem.at[2 * f + n]
-            )
-            store.start()
-            stores.append(store)
 
     for c in sends:
         c.wait_send()
@@ -309,6 +307,11 @@
         for c in hands:
             c.wait_send()
 
+
+def write_out(o, out, sem):
+    stores = [pltpu.make_async_copy(o.at[f], out.at[f], sem.at[f]) for f in range(o.shape[0])]
+    for c in stores:
+        c.start()
     for c in stores:
         c.wait()
 
@@ -318,13 +321,13 @@
     pairs = rows // 2 + 1
     span = rows + 2 * TOP
     tall = rows + 16
-    anywhere = pl.BlockSpec(memory_space=pl.ANY)
+    hbm = pl.BlockSpec(memory_space=pltpu.HBM)
     vmem = pl.BlockSpec(memory_space=pltpu.VMEM)
     out = pl.pallas_call(
         functools.partial(kernel, TROWS),
-        out_shape=jax.ShapeDtypeStruct((count, rows // 2, 2, cols, C), BF),
-        in_specs=[anywhere, anywhere, anywhere, vmem, vmem],
-        out_specs=anywhere,
+        out_shape=pltpu.VMEM((count, rows // 2, 2, cols, C), BF),
+        in_specs=[hbm] * 5,
+        out_specs=vmem,
         scratch_shapes=[
             pltpu.VMEM((count, rows + 4, cols, C), BF),
             pltpu.VMEM((count, rows + 4, cols, 3 * C), BF),
@@ -344,19 +347,27 @@
             pltpu.VMEM((pairs, 2, cols, C), BF),
             pltpu.VMEM((2, 2, tall, C), BF),
             pltpu.VMEM((2, 2, tall, C), BF),
-            pltpu.VMEM((count, rows // 2, 2, cols, C), BF),
+            pltpu.VMEM((count, C), F32),
+            pltpu.VMEM((1, C), F32),
             pltpu.SemaphoreType.DMA((count,)),
-            pltpu.SemaphoreType.DMA((2,)),
+            pltpu.SemaphoreType.DMA((4,)),
             pltpu.SemaphoreType.DMA((10,)),
             pltpu.SemaphoreType.DMA((10,)),
             pltpu.SemaphoreType.DMA((5,)),
             pltpu.SemaphoreType.DMA((5,)),
-            pltpu.SemaphoreType.DMA((2 * count,)),
         ],
         compiler_params=pltpu.CompilerParams(
-            collective_id=0, has_side_effects=True, vmem_limit_bytes=56 * 2**20
+            collective_id=0, has_side_effects=True, vmem_limit_bytes=44 * 2**20
         ),
-    )(frames[:, 0], w_in, w_out, decay, skip.reshape(1, C))
+    )(*(pltpu.with_memory_space_constraint(a, pltpu.HBM) for a in (frames[:, 0], w_in, w_out, decay, skip.reshape(1, C))))
+    out = pl.pallas_call(
+        write_out,
+        out_shape=jax.ShapeDtypeStruct(out.shape, BF),
+        in_specs=[vmem],
+        out_specs=hbm,
+        scratch_shapes=[pltpu.SemaphoreType.DMA((count,))],
+        compiler_params=pltpu.CompilerParams(vmem_limit_bytes=2**20),
+    )(pltpu.with_memory_space_constraint(out, pltpu.VMEM))
     return out.reshape(count, 1, rows, cols, C)
 
 

time: 30.7 us -> 27 us (0.88)
  local copies, waits for them, and re-layouts: 3.35 us -> 0 us
    unnamed x1 -> x0, local copies, waits for them, and re-layouts: 3.35 us -> none
    pallas_call x1 -> x2, Pallas kernels: 27.1 us -> 26.8 us  [the longest x1 25.5 us: per_device(): pl.pallas_call(functools.partial(kernel, TROWS), out_shape=pltpu.VMEM((co...]
where the time goes in v2:
time: 27 us; the launch traced here: 26.9 us
  Pallas kernels  26.8 us (99%)
    pallas_call x1, Pallas kernels, per_device(): pl.pallas_call(functools.partial(kernel, TROWS), out_shape=pltpu.VMEM((co...  25.5 us
    pallas_call x1, Pallas kernels, per_device(): pl.pallas_call(write_out, out_shape=jax.ShapeDtypeStruct(out.shape, BF),...  1.35 us

profile of v2, /device:TPU:1, one launch (start us, length us, event | category | flops | bytes accessed | tf_op | source)
XLA Modules:
  0.0 26.9 jit_solution(13120152130679527216)
XLA Ops:
  0.0 25.5 %shard_map.55.o = bf16[4,32,2,32,128]{4,3,2,1,0:T(8,128)(2,1)S(1)} custom-call(bf16[4,64,32,128]{3,2,1,0:T(8,128)(2,1)} %bitcast.5, bf16[3,3,128,128]{3,2,1,0:T(8,128)(2,1)} %w_in.1, bf16[3,3,128,128]{3,2,1,0:T(8,128)(2,1)} %w_out.1, f32[4,128]{1,0:T(4,128)} %decay_in.1, f32[1,128]{1,0:T(1,128)} %bitcast.6), custom_call_target="tpu_custom_call" | custom-call | tf_op jit(solution)/shard_map/pallas_call | solution.py:326
  25.5 1.3 %shard_map.56 = bf16[4,32,2,32,128]{4,3,2,1,0:T(8,128)(2,1)} custom-call(bf16[4,32,2,32,128]{4,3,2,1,0:T(8,128)(2,1)S(1)} %shard_map.55.o), custom_call_target="tpu_custom_call" | custom-call | tf_op jit(solution)/shard_map/pallas_call | solution.py:363

commit v3 on v2

v3 whole, which is shorter than its diff:
```python
import functools

import jax
import jax.numpy as jnp
from jax import lax
from jax.experimental import pallas as pl
from jax.experimental.pallas import tpu as pltpu
from jax.sharding import PartitionSpec as P

TROWS = 4
C = 128
BF = jnp.bfloat16
F32 = jnp.float32
MESH = pl.DeviceIdType.MESH

TOP = 16
TAPS = (0, 2, 1)


def mm(lhs, rhs):
    return jnp.dot(lhs, rhs, preferred_element_type=F32)


def pair_weights(w, pair):
    zero = jnp.zeros((C, C), BF)
    for i in range(4):
        for n, b in enumerate(TAPS):
            rows = pl.ds((i * 3 + n) * C, C)
            pair[rows, 0:C] = w[i, b] if i < 3 else zero
            pair[rows, C : 2 * C] = w[i - 1, b] if i > 0 else zero


def side_weights(w, side, table):
    zero = jnp.zeros((C, C), BF)
    for s in range(2):
        for a in range(3):
            for k, taps in enumerate(table[s]):
                for e, b in enumerate(taps):
                    lanes = pl.ds((a * 2 + e) * C, C)
                    side[s, pl.ds(k * C, C), lanes] = zero if b is None else w[a, b]


SIDE_IN = (((1, 0), (0, None), (2, None)), ((1, 2), (2, None), (0, None)))
SIDE_OUT = (((0, None), (1, 0)), ((2, None), (1, 2)))


def pair_rows(parts, pairs):
    cols = parts[0].shape[1]
    split = [p.reshape(pairs + 1, 2, cols, p.shape[2]) for p in parts]
    taps = []
    for first in (0, 1):
        for parity in (0, 1):
            taps += [p[first : first + pairs, parity] for p in split]
    return jnp.concatenate(taps, axis=-1).reshape(pairs * cols, 12 * C)


def kernel(
    trows, frames, w_in, w_out, decay_in, skip_in, o,
    x, x3, s3, loc, w1, w2, pw1, pw2, sw1, sw2, edge, z, y, y2, ss, own, stage, lo, inc, so, si, ot, decay, skip,
    load_sem, w_sem, send_sem, recv_sem, tsend_sem, trecv_sem,
):
    count, rows, cols, _ = frames.shape
    tiles = lax.axis_size("tile")
    tcols = tiles // trows
    me = lax.axis_index("tile")
    tm = lax.axis_index("tm")
    k = lax.rem(me + tiles - 1, tiles)
    column = lax.rem(k, tcols)
    row_index = k // tcols
    at_top = row_index == 0
    at_bottom = row_index == trows - 1
    pairs = rows // 2
    tall = rows + 16
    span = rows + 2 * TOP

    loads = [
        pltpu.make_async_copy(frames.at[f], x.at[f, pl.ds(2, rows)], load_sem.at[f])
        for f in range(count)
    ]
    for c in loads:
        c.start()
    wloads = [
        pltpu.make_async_copy(src, dst, w_sem.at[i])
        for i, (src, dst) in enumerate(((w_in, w1), (decay_in, decay), (skip_in, skip), (w_out, w2)))
    ]
    for c in wloads:
        c.start()

    def at(by):
        return lax.rem(me + by + tiles, tiles)

    barrier = pltpu.get_barrier_semaphore()
    steps = (-1, 1, -tcols, tcols, -tcols - 1, -tcols + 1, tcols - 1, tcols + 1)
    for by in steps:
        pl.semaphore_signal(barrier, inc=1, device_id=(tm, at(by)), device_id_type=MESH)
    pl.semaphore_signal(barrier, inc=1, device_id=(1 - tm, me), device_id_type=MESH)

    own[:, :, 0:8] = jnp.zeros((2, count, 8, C), F32)
    own[:, :, rows + 8 : rows + 16] = jnp.zeros((2, count, 8, C), F32)

    for f in range(count):
        loads[f].wait()
        first = x[f, 2 : 2 + rows, 0:16, :].astype(F32)[:, 0:8, :]
        stage[0] = first.reshape(rows * 8, C)
        last = x[f, 2 : 2 + rows, cols - 16 : cols, :].astype(F32)[:, 8:16, :]
        stage[1] = last.reshape(rows * 8, C)
        for s in range(2):
            for n in range(2):
                offset = n if s == 0 else 7 - n
                value = stage[s, pl.ds(offset, rows, stride=8), :].astype(BF)
                edge[s, n, f] = value
                if n == 0:
                    z[s, 2, f, TOP : TOP + rows] = value

    pl.semaphore_wait(barrier, 9)

    low, mid, high = pl.ds(0, TOP), pl.ds(TOP, rows), pl.ds(TOP + rows, TOP)
    head, tail = pl.ds(0, TOP), pl.ds(rows - TOP, TOP)
    two = pl.ds(0, 2)
    plan = [
        (edge.at[0], z.at[1, two, :, mid], -1),
        (edge.at[1], z.at[0, two, :, mid], 1),
        (frames.at[:, pl.ds(0, 2)], x.at[:, pl.ds(rows + 2, 2)], -tcols),
        (frames.at[:, pl.ds(rows - 2, 2)], x.at[:, pl.ds(0, 2)], tcols),
        (edge.at[:, 0, :, head], z.at[:, 2, :, high], -tcols),
        (edge.at[:, 0, :, tail], z.at[:, 2, :, low], tcols),
        (edge.at[0, :, :, head], z.at[1, two, :, high], -tcols - 1),
        (edge.at[1, :, :, head], z.at[0, two, :, high], -tcols + 1),
        (edge.at[0, :, :, tail], z.at[1, two, :, low], tcols - 1),
        (edge.at[1, :, :, tail], z.at[0, two, :, low], tcols + 1),
    ]
    sends = [
        pltpu.make_async_remote_copy(
            src_ref=src, dst_ref=dst, send_sem=send_sem.at[i], recv_sem=recv_sem.at[i],
            device_id=(tm, at(by)), device_id_type=MESH,
        )
        for i, (src, dst, by) in enumerate(plan)
    ]
    for c in sends:
        c.start()

    for c in wloads[:3]:
        c.wait()
    pair_weights(w1, pw1)

    in_tile = lax.broadcasted_iota(jnp.int32, (1, 8, C), 1)

    def shifted(wide):
        no_last = jnp.concatenate([wide[:, : cols - 8], jnp.where(in_tile == 7, 0.0, wide[:, cols - 8 :])], axis=1)
        no_first = jnp.concatenate([jnp.where(in_tile == 0, 0.0, wide[:, :8]), wide[:, 8:]], axis=1)
        return pltpu.roll(no_last, 1, 1), pltpu.roll(no_first, cols - 1, 1)

    def widen(f, start, size, real=None):
        wide = x[f, pl.ds(start, size)].astype(F32)
        if real is not None:
            wide = jnp.where(real, wide, 0.0)
            x[f, pl.ds(start, size)] = wide.astype(BF)
        left, right = shifted(wide)
        x3[f, pl.ds(start, size), :, 0:C] = left.astype(BF)
        x3[f, pl.ds(start, size), :, C : 2 * C] = right.astype(BF)

    def exchange(i, src, dst):
        return pltpu.make_async_remote_copy(
            src_ref=src, dst_ref=dst, send_sem=tsend_sem.at[i], recv_sem=trecv_sem.at[i],
            device_id=(1 - tm, me), device_id_type=MESH,
        )

    half = pairs // 2
    chunks = [(1, half), (1 + half, pairs - 1 - half)]
    hands = [exchange(n, lo.at[pl.ds(q, size)], inc.at[pl.ds(q, size)]) for n, (q, size) in enumerate(chunks)]
    late_hands = [
        exchange(2, lo.at[pl.ds(0, 1)], inc.at[pl.ds(0, 1)]),
        exchange(3, lo.at[pl.ds(pairs, 1)], inc.at[pl.ds(pairs, 1)]),
        exchange(4, so, si),
    ]

    def recur(f, q, size, drive):
        drive = drive.reshape(size, cols, 2 * C)
        drive = jnp.stack([drive[:, :, :C], drive[:, :, C:]], axis=1).reshape(size * 2 * cols, C)
        here = pl.ds(q * 2 * cols, size * 2 * cols)
        if f > 0:
            drive = decay[f : f + 1, :] * loc[f - 1, here] + drive
        loc[f, here] = drive
        if f == count - 1:
            lo[pl.ds(q, size)] = drive.astype(BF).reshape(size, 2, cols, C)

    for n, (q, size) in enumerate(chunks):
        for f in range(count):
            end = rows + 2 if n else 2 * half + 4
            for start in range(2 + n * (2 * half + 2), end, 2):
                widen(f, start, 2)
            here = pl.ds(2 * q, 2 * size + 2)
            lhs = pair_rows([x3[f, here], x[f, here]], size)
            recur(f, q, size, mm(lhs, pw1[...]))
        hands[n].start()

    factors = []
    for f in range(count):
        keep = decay[f : f + 1, :]
        factors.append(keep * jnp.where(tm == 0, 0.0, 1.0) if f == 0 else factors[-1] * keep)

    def settle(f, q, real=(None, None)):
        state = loc[f, pl.ds(q * 2 * cols, 2 * cols)].reshape(2, cols, C) + factors[f] * inc[q].astype(F32)
        first = jnp.where(in_tile == 0, 0.0, state[:, :8])
        last = jnp.where(in_tile == 7, 0.0, state[:, cols - 8 :])
        state = jnp.concatenate([first, state[:, 8 : cols - 8], last], axis=1)
        state = jnp.concatenate(
            [state[e : e + 1] if r is None else jnp.where(r, state[e : e + 1], 0.0) for e, r in enumerate(real)],
            axis=0,
        )
        here = pl.ds(2 * q, 2)
        s3[f, here, :, 0:C] = pltpu.roll(state, 1, 1).astype(BF)
        s3[f, here, :, C : 2 * C] = pltpu.roll(state, cols - 1, 1).astype(BF)
        s3[f, here, :, 2 * C : 3 * C] = state.astype(BF)

    def finish(f, p, size, result):
        result = result.reshape(size, cols, 2 * C)
        result = jnp.stack([result[:, :, :C], result[:, :, C:]], axis=1).reshape(2 * size, cols, C)
        mixed = result + skip[...] * x[f, pl.ds(2 + 2 * p, 2 * size)].astype(F32)
        ot[0, f, pl.ds(16 * p, 16 * size)] = mixed[:, :8].reshape(16 * size, C)
        ot[1, f, pl.ds(16 * p, 16 * size)] = mixed[:, cols - 8 :].reshape(16 * size, C)
        o[f, pl.ds(2 * p, 2 * size), 8 : cols - 8] = mixed[:, 8 : cols - 8].astype(BF)

    wloads[3].wait()
    pair_weights(w2, pw2)
    side_weights(w1, sw1, SIDE_IN)
    side_weights(w2, sw2, SIDE_OUT)
    for c in hands:
        c.wait_recv()
    inner = [(1, half - 1), (half, half - 1)]
    for f in range(count):
        for q in range(1, pairs):
            settle(f, q)
        for p, size in inner:
            finish(f, p, size, mm(pair_rows([s3[f, 2 * p : 2 * p + 2 * size + 2]], size), pw2[...]))

    for c in sends:
        c.wait_recv()
    for s in range(2):
        lhs = jnp.concatenate([z[s, n].reshape(count * span, C) for n in range(3)], axis=-1)
        result = mm(lhs, sw1[s])
        for a in range(3):
            y[s, a] = result[:, a * 2 * C : (a + 1) * 2 * C].reshape(count, span, 2 * C)
    for f in range(count):
        widen(f, 0, 2, jnp.logical_not(at_top))
        widen(f, rows + 2, 2, jnp.logical_not(at_bottom))
    lhs = [
        pair_rows([x3[f, 2 * q : 2 * q + 4], x[f, 2 * q : 2 * q + 4]], 1) for q in (0, pairs) for f in range(count)
    ]
    drive = mm(jnp.concatenate(lhs, axis=0), pw1[...])
    for n, q in enumerate((0, pairs)):
        for f in range(count):
            recur(f, q, 1, drive[(n * count + f) * cols : (n * count + f + 1) * cols])
    late_hands[0].start()
    late_hands[1].start()

    @pl.when(at_top)
    def _():
        y[:, 0, :, 8:TOP] = jnp.zeros((2, count, TOP - 8, 2 * C), F32)

    @pl.when(at_bottom)
    def _():
        y[:, 2, :, TOP + rows : TOP + rows + 8] = jnp.zeros((2, count, 8, 2 * C), F32)

    for s in range(2):
        inside = jnp.where(column > 0 if s == 0 else column < tcols - 1, 1.0, 0.0).astype(F32)
        for f in range(count):
            own[s, f, 7 : rows + 9] = loc[f, pl.ds(s * (cols - 1), rows + 2, stride=cols), :]
        for e in range(2):
            lanes = slice(e * C, (e + 1) * C)
            state = None
            for f in range(count):
                drive = (
                    y[s, 0, f, 7 : 7 + tall, lanes] + y[s, 1, f, 8 : 8 + tall, lanes] + y[s, 2, f, 9 : 9 + tall, lanes]
                ) * inside
                state = drive if f == 0 else decay[f : f + 1, :] * state + drive
                whole = state + own[s, f] if e == 1 else state
                ss[s, e, f] = whole
            so[s, e] = whole.astype(BF)
    late_hands[2].start()
    for c in late_hands:
        c.wait_recv()

    place = lax.broadcasted_iota(jnp.int32, (tall, C), 0)
    off = jnp.logical_or(
        jnp.logical_and(place == 7, at_top), jnp.logical_and(place == rows + 8, at_bottom)
    )
    for s in range(2):
        sides = []
        for f in range(count):
            both = [
                jnp.where(off, 0.0, ss[s, e, f] + factors[f] * si[s, e].astype(F32)).astype(BF) for e in range(2)
            ]
            sides.append(jnp.concatenate(both, axis=-1))
        result = mm(jnp.concatenate(sides, axis=0), sw2[s])
        for a in range(3):
            y2[s, a] = result[:, a * 2 * C : (a + 1) * 2 * C].reshape(count, tall, 2 * C)
    for f in range(count):
        settle(f, 0, (jnp.logical_not(at_top), None))
        settle(f, pairs, (None, jnp.logical_not(at_bottom)))
    lhs = [pair_rows([s3[f, 2 * p : 2 * p + 4]], 1) for p in (0, pairs - 1) for f in range(count)]
    result = mm(jnp.concatenate(lhs, axis=0), pw2[...])
    for n, p in enumerate((0, pairs - 1)):
        for f in range(count):
            finish(f, p, 1, result[(n * count + f) * cols : (n * count + f + 1) * cols])

    for f in range(count):
        for s in range(2):
            for e in range(2):
                lanes = slice(e * C, (e + 1) * C)
                here = pl.ds(e if s == 0 else 7 - e, rows, stride=8)
                fix = (
                    y2[s, 0, f, 7 : 7 + rows, lanes] + y2[s, 1, f, 8 : 8 + rows, lanes] + y2[s, 2, f, 9 : 9 + rows, lanes]
                )
                ot[s, f, here, :] = ot[s, f, here, :] + fix
        o[f, :, 0:8] = ot[0, f].reshape(rows, 8, C).astype(BF)
        o[f, :, cols - 8 :] = ot[1, f].reshape(rows, 8, C).astype(BF)

    for c in sends + hands + late_hands:
        c.wait_send()


def write_out(o, out, sem):
    stores = [pltpu.make_async_copy(o.at[f], out.at[f], sem.at[f]) for f in range(o.shape[0])]
    for c in stores:
        c.start()
    for c in stores:
        c.wait()


def per_device(frames, w_in, w_out, decay, skip):
    count, _, rows, cols, _ = frames.shape
    pairs = rows // 2
    span = rows + 2 * TOP
    tall = rows + 16
    hbm = pl.BlockSpec(memory_space=pltpu.HBM)
    vmem = pl.BlockSpec(memory_space=pltpu.VMEM)
    args = (frames[:, 0], w_in, w_out, decay, skip.reshape(1, C))
    out = pl.pallas_call(
        functools.partial(kernel, TROWS),
        out_shape=pltpu.VMEM((count, rows, cols, C), BF),
        in_specs=[hbm] * 5,
        out_specs=vmem,
        scratch_shapes=[
            pltpu.VMEM((count, rows + 4, cols, C), BF),
            pltpu.VMEM((count, rows + 4, cols, 2 * C), BF),
            pltpu.VMEM((count, rows + 2, cols, 3 * C), BF),
            pltpu.VMEM((count, (rows + 8) * cols, C), F32),
            pltpu.VMEM((3, 3, C, C), BF),
            pltpu.VMEM((3, 3, C, C), BF),
            pltpu.VMEM((12 * C, 2 * C), BF),
            pltpu.VMEM((12 * C, 2 * C), BF),
            pltpu.VMEM((2, 3 * C, 6 * C), BF),
            pltpu.VMEM((2, 2 * C, 6 * C), BF),
            pltpu.VMEM((2, 2, count, rows, C), BF),
            pltpu.VMEM((2, 3, count, span, C), BF),
            pltpu.VMEM((2, 3, count, span, 2 * C), F32),
            pltpu.VMEM((2, 3, count, tall, 2 * C), F32),
            pltpu.VMEM((2, 2, count, tall, C), F32),
            pltpu.VMEM((2, count, tall, C), F32),
            pltpu.VMEM((2, rows * 8, C), F32),
            pltpu.VMEM((pairs + 1, 2, cols, C), BF),
            pltpu.VMEM((pairs + 1, 2, cols, C), BF),
            pltpu.VMEM((2, 2, tall, C), BF),
            pltpu.VMEM((2, 2, tall, C), BF),
            pltpu.VMEM((2, count, rows * 8, C), F32),
            pltpu.VMEM((count, C), F32),
            pltpu.VMEM((1, C), F32),
            pltpu.SemaphoreType.DMA((count,)),
            pltpu.SemaphoreType.DMA((4,)),
            pltpu.SemaphoreType.DMA((10,)),
            pltpu.SemaphoreType.DMA((10,)),
            pltpu.SemaphoreType.DMA((5,)),
            pltpu.SemaphoreType.DMA((5,)),
        ],
        compiler_params=pltpu.CompilerParams(
            collective_id=0, has_side_effects=True, vmem_limit_bytes=48 * 2**20
        ),
    )(*(pltpu.with_memory_space_constraint(a, pltpu.HBM) for a in args))
    out = pl.pallas_call(
        write_out,
        out_shape=jax.ShapeDtypeStruct(out.shape, BF),
        in_specs=[vmem],
        out_specs=hbm,
        scratch_shapes=[pltpu.SemaphoreType.DMA((count,))],
        compiler_params=pltpu.CompilerParams(vmem_limit_bytes=2**20),
    )(pltpu.with_memory_space_constraint(out, pltpu.VMEM))
    return out.reshape(count, 1, rows, cols, C)


def solution(mesh):
    return jax.shard_map(
        per_device,
        mesh=mesh,
        in_specs=(P("tm", "tile", None, None, None), P(), P(), P("tm", None), P()),
        out_specs=P("tm", "tile", None, None, None),
        check_vma=False,
    )
```

time: 27 us -> 24.2 us (0.90)
  Pallas kernels: 26.8 us -> 24.1 us
    pallas_call x1, Pallas kernels: 25.5 us -> 22.7 us  [per_device(): pl.pallas_call(functools.partial(kernel, TROWS), out_shape=pltpu.VMEM((co...]
where the time goes in v3:
time: 24.2 us; the launch traced here: 24.1 us
  Pallas kernels  24.1 us (100%)
    pallas_call x1, Pallas kernels, per_device(): pl.pallas_call(functools.partial(kernel, TROWS), out_shape=pltpu.VMEM((co...  22.7 us
    pallas_call x1, Pallas kernels, per_device(): pl.pallas_call(write_out, out_shape=jax.ShapeDtypeStruct(out.shape, BF),...  1.35 us

profile of v3, /device:TPU:1, one launch (start us, length us, event | category | flops | bytes accessed | tf_op | source)
XLA Modules:
  0.0 24.1 jit_solution(2098125731559786794)
XLA Ops:
  0.0 22.7 %shard_map.55.o = bf16[4,64,32,128]{3,2,1,0:T(8,128)(2,1)S(1)} custom-call(bf16[4,64,32,128]{3,2,1,0:T(8,128)(2,1)} %bitcast.5, bf16[3,3,128,128]{3,2,1,0:T(8,128)(2,1)} %w_in.1, bf16[3,3,128,128]{3,2,1,0:T(8,128)(2,1)} %w_out.1, f32[4,128]{1,0:T(4,128)} %decay_in.1, f32[1,128]{1,0:T(1,128)} %bitcast.6), custom_call_target="tpu_custom_call" | custom-call | tf_op jit(solution)/shard_map/pallas_call | solution.py:339
  22.7 1.3 %shard_map.56 = bf16[4,64,32,128]{3,2,1,0:T(8,128)(2,1)} custom-call(bf16[4,64,32,128]{3,2,1,0:T(8,128)(2,1)S(1)} %shard_map.55.o), custom_call_target="tpu_custom_call" | custom-call | tf_op jit(solution)/shard_map/pallas_call | solution.py:380

commit v4 on v3

v4 whole, which is shorter than its diff:
```python
import functools

import jax
import jax.numpy as jnp
from jax import lax
from jax.experimental import pallas as pl
from jax.experimental.pallas import tpu as pltpu
from jax.sharding import PartitionSpec as P

TROWS = 4
C = 128
BF = jnp.bfloat16
F32 = jnp.float32
MESH = pl.DeviceIdType.MESH

TAPS = 3


def mm(lhs, rhs):
    return jnp.dot(lhs, rhs, preferred_element_type=F32)


def mm_halves(lhs, rhs):
    half = lhs.shape[1] // 2
    return mm(lhs[:, :half], rhs[:half]) + mm(lhs[:, half:], rhs[half:])


def pair_weights(w, pair):
    zero = jnp.zeros((TAPS, C, C), BF)
    pair[3 * TAPS : 4 * TAPS, :, 0:C] = zero
    pair[0:TAPS, :, C : 2 * C] = zero
    return [
        (w.at[i], pair.at[pl.ds((i + e) * TAPS, TAPS), :, pl.ds(e * C, C)]) for i in range(TAPS) for e in range(2)
    ]


def side_weights(w, side, table):
    copies = []
    for s in range(2):
        for k, taps in enumerate(table[s]):
            for e, b in enumerate(taps):
                if b is None:
                    side[s, :, k, :, e * C : (e + 1) * C] = jnp.zeros((TAPS, C, C), BF)
                else:
                    copies.append((w.at[:, b], side.at[s, :, k, :, pl.ds(e * C, C)]))
    return copies


SIDE_IN = (((1, 0), (0, None), (2, None)), ((1, 2), (2, None), (0, None)))
SIDE_OUT = (((0, None), (1, 0)), ((2, None), (1, 2)))


def pair_rows(parts, pairs):
    cols = parts[0].shape[1]
    split = [p.reshape(pairs + 1, 2, cols, p.shape[2]) for p in parts]
    taps = []
    for first in (0, 1):
        for parity in (0, 1):
            taps += [p[first : first + pairs, parity] for p in split]
    return jnp.concatenate(taps, axis=-1).reshape(pairs * cols, 12 * C)


def kernel(
    trows, frames, w_in, w_out, decay_in, skip_in, o,
    x, x3, s3, loc, pw1, pw2, sw1, sw2, edge, corner, z, zc, y, y2, ss, stage, cstage, rim, lo, inc, so, si, ot, decay, skip,
    load_sem, w_sem, send_sem, recv_sem, tsend_sem, trecv_sem,
):
    count, rows, cols, _ = frames.shape
    tiles = lax.axis_size("tile")
    tcols = tiles // trows
    me = lax.axis_index("tile")
    tm = lax.axis_index("tm")
    k = lax.rem(me + tiles - 1, tiles)
    column = lax.rem(k, tcols)
    row_index = k // tcols
    up, down = row_index > 0, row_index < trows - 1
    left, right = column > 0, column < tcols - 1
    pairs = rows // 2
    tall = rows + 16

    loads = [
        pltpu.make_async_copy(frames.at[f], x.at[f, pl.ds(2, rows)], load_sem.at[f])
        for f in range(count)
    ]
    for c in loads:
        c.start()

    both = jnp.logical_and
    around = [
        (-1, left), (1, right), (-tcols, up), (tcols, down),
        (-tcols - 1, both(up, left)), (-tcols + 1, both(up, right)),
        (tcols - 1, both(down, left)), (tcols + 1, both(down, right)),
    ]

    def at(by):
        return lax.rem(me + by + tiles, tiles)

    barrier = pltpu.get_barrier_semaphore()
    greeted = jnp.int32(1)
    for by, there in around:
        greeted = greeted + there.astype(jnp.int32)

        @pl.when(there)
        def _():
            pl.semaphore_signal(barrier, inc=1, device_id=(tm, at(by)), device_id_type=MESH)

    pl.semaphore_signal(barrier, inc=1, device_id=(1 - tm, me), device_id_type=MESH)

    placed = pair_weights(w_in, pw1) + [(decay_in, decay), (skip_in, skip)]
    first_needed = len(placed)
    placed += pair_weights(w_out, pw2)
    then_needed = len(placed)
    placed += side_weights(w_in, sw1, SIDE_IN) + side_weights(w_out, sw2, SIDE_OUT)
    placed = [pltpu.make_async_copy(src, dst, w_sem.at[i]) for i, (src, dst) in enumerate(placed)]
    for c in placed:
        c.start()

    for f in range(count):
        loads[f].wait()
        stage[0] = x[f, 2 : 2 + rows, 0:16, :].astype(F32)[:, 0:8, :].reshape(rows * 8, C)
        stage[1] = x[f, 2 : 2 + rows, cols - 16 : cols, :].astype(F32)[:, 8:16, :].reshape(rows * 8, C)
        for s in range(2):
            for n in range(2):
                offset = n if s == 0 else 7 - n
                edge[s, n, f] = stage[s, pl.ds(offset, rows, stride=8), :].astype(BF)
                for t in range(2):
                    ends = pl.ds(offset + t * (rows - 2) * 8, 2, stride=8)
                    cstage[s, t, n, 2 * f : 2 * f + 2] = stage[s, ends, :]
    rest = jnp.zeros((8, C), F32)
    for s in range(2):
        for t in range(2):
            for n in range(2):
                corner[s, t, n] = jnp.concatenate([cstage[s, t, n], rest], axis=0).astype(BF)

    plan = [
        (edge.at[0], z.at[1]),
        (edge.at[1], z.at[0]),
        (frames.at[:, pl.ds(0, 2)], x.at[:, pl.ds(rows + 2, 2)]),
        (frames.at[:, pl.ds(rows - 2, 2)], x.at[:, pl.ds(0, 2)]),
        (corner.at[0, 0], zc.at[1, 1]),
        (corner.at[1, 0], zc.at[0, 1]),
        (corner.at[0, 1], zc.at[1, 0]),
        (corner.at[1, 1], zc.at[0, 0]),
    ]
    sends = [
        pltpu.make_async_remote_copy(
            src_ref=src, dst_ref=dst, send_sem=send_sem.at[i], recv_sem=recv_sem.at[i],
            device_id=(tm, at(around[i][0])), device_id_type=MESH,
        )
        for i, (src, dst) in enumerate(plan)
    ]
    comes = [around[i ^ 1][1] if i < 4 else around[11 - i][1] for i in range(8)]
    for i, (_, dst) in enumerate(plan):
        @pl.when(jnp.logical_not(comes[i]))
        def _():
            dst[...] = jnp.zeros(dst.shape, BF)

    in_tile = lax.broadcasted_iota(jnp.int32, (1, 8, C), 1)

    def widen(f, start, size):
        wide = x[f, pl.ds(start, size)].astype(F32)
        no_last = jnp.concatenate([wide[:, : cols - 8], jnp.where(in_tile == 7, 0.0, wide[:, cols - 8 :])], axis=1)
        no_first = jnp.concatenate([jnp.where(in_tile == 0, 0.0, wide[:, :8]), wide[:, 8:]], axis=1)
        x3[f, pl.ds(start, size), :, 0:C] = pltpu.roll(no_last, 1, 1).astype(BF)
        x3[f, pl.ds(start, size), :, C : 2 * C] = pltpu.roll(no_first, cols - 1, 1).astype(BF)
        return wide

    def frame_rows(f, here):
        return [x3[f, here, :, 0:C], x[f, here], x3[f, here, :, C : 2 * C]]

    def exchange(i, src, dst):
        return pltpu.make_async_remote_copy(
            src_ref=src, dst_ref=dst, send_sem=tsend_sem.at[i], recv_sem=trecv_sem.at[i],
            device_id=(1 - tm, me), device_id_type=MESH,
        )

    half = pairs // 2
    chunks = [(1, half), (1 + half, pairs - 1 - half)]
    hands = [exchange(n, lo.at[pl.ds(q, size)], inc.at[pl.ds(q, size)]) for n, (q, size) in enumerate(chunks)]
    late_hands = [
        exchange(2, lo.at[pl.ds(0, 1)], inc.at[pl.ds(0, 1)]),
        exchange(3, lo.at[pl.ds(pairs, 1)], inc.at[pl.ds(pairs, 1)]),
        exchange(4, so, si),
    ]
    weights1 = pw1.reshape(4 * TAPS * C, 2 * C)
    weights2 = pw2.reshape(4 * TAPS * C, 2 * C)

    def loc_rows(q, size):
        return pl.ds((2 * q + 7) * cols, size * 2 * cols)

    def recur(f, q, size, drive):
        drive = drive.reshape(size, cols, 2 * C)
        drive = jnp.stack([drive[:, :, :C], drive[:, :, C:]], axis=1).reshape(size * 2 * cols, C)
        here = loc_rows(q, size)
        if f > 0:
            drive = decay[f : f + 1, :] * loc[f - 1, here] + drive
        loc[f, here] = drive
        if f == count - 1:
            lo[pl.ds(q, size)] = drive.astype(BF).reshape(size, 2, cols, C)

    greet_at = jnp.where(me == 0, 1, 0)

    @pl.loop(0, 2)
    def _(step):
        @pl.when(step == greet_at)
        def _():
            pl.semaphore_wait(barrier, greeted)
            for i, c in enumerate(sends):
                pl.when(around[i][1])(c.start)

        @pl.when(step != greet_at)
        def _():
            for c in placed[:first_needed]:
                c.wait()
            for n, (q, size) in enumerate(chunks):
                for f in range(count):
                    end = rows + 2 if n else 2 * half + 4
                    for start in range(2 + n * (2 * half + 2), end, 2):
                        widen(f, start, 2)
                    lhs = pair_rows(frame_rows(f, pl.ds(2 * q, 2 * size + 2)), size)
                    recur(f, q, size, mm(lhs, weights1[...]))
                if n == 0:
                    pl.when(greet_at == 0)(hands[0].start)

    pl.when(greet_at == 1)(hands[0].start)
    hands[1].start()

    factors = []
    for f in range(count):
        keep = decay[f : f + 1, :]
        factors.append(keep * jnp.where(tm == 0, 0.0, 1.0) if f == 0 else factors[-1] * keep)

    def settle(f, q, real=(None, None)):
        state = loc[f, loc_rows(q, 1)].reshape(2, cols, C) + factors[f] * inc[q].astype(F32)
        first = jnp.where(in_tile == 0, 0.0, state[:, :8])
        last = jnp.where(in_tile == 7, 0.0, state[:, cols - 8 :])
        state = jnp.concatenate([first, state[:, 8 : cols - 8], last], axis=1)
        state = jnp.concatenate(
            [state[e : e + 1] if r is None else jnp.where(r, state[e : e + 1], 0.0) for e, r in enumerate(real)],
            axis=0,
        )
        here = pl.ds(2 * q, 2)
        s3[f, here, :, 0:C] = pltpu.roll(state, 1, 1).astype(BF)
        s3[f, here, :, C : 2 * C] = state.astype(BF)
        s3[f, here, :, 2 * C : 3 * C] = pltpu.roll(state, cols - 1, 1).astype(BF)

    def finish(f, p, size, result):
        result = result.reshape(size, cols, 2 * C)
        result = jnp.stack([result[:, :, :C], result[:, :, C:]], axis=1).reshape(2 * size, cols, C)
        mixed = result + skip[...] * x[f, pl.ds(2 + 2 * p, 2 * size)].astype(F32)
        ot[0, f, pl.ds(16 * p, 16 * size)] = mixed[:, :8].reshape(16 * size, C)
        ot[1, f, pl.ds(16 * p, 16 * size)] = mixed[:, cols - 8 :].reshape(16 * size, C)
        o[f, pl.ds(2 * p, 2 * size), 8 : cols - 8] = mixed[:, 8 : cols - 8].astype(BF)

    for c in placed[first_needed:then_needed]:
        c.wait()
    inner = [(1, half - 1), (half, half - 1)]
    for n, (q, size) in enumerate(chunks):
        hands[n].wait_recv()
        p, deep = inner[n]
        for f in range(count):
            for i in range(q, q + size):
                settle(f, i)
            lhs = pair_rows([s3[f, 2 * p : 2 * p + 2 * deep + 2]], deep)
            finish(f, p, deep, mm(lhs, weights2[...]))

    for c in placed[then_needed:]:
        c.wait()
    for i, c in enumerate(sends):
        pl.when(comes[i])(c.wait_recv)
    for f in range(count):
        for t in range(2):
            wide = widen(f, t * (rows + 2), 2)
            rim[t, 0, 16 * f : 16 * f + 16] = wide[:, :8].reshape(16, C)
            rim[t, 1, 16 * f : 16 * f + 16] = wide[:, cols - 8 :].reshape(16, C)
    lhs = [pair_rows(frame_rows(f, pl.ds(2 * q, 4)), 1) for q in (0, pairs) for f in range(count)]
    drive = mm_halves(jnp.concatenate(lhs, axis=0), weights1[...])
    for n, q in enumerate((0, pairs)):
        for f in range(count):
            recur(f, q, 1, drive[(n * count + f) * cols : (n * count + f + 1) * cols])
    late_hands[0].start()
    late_hands[1].start()

    for s in range(2):
        lines = [jnp.concatenate([z[s, 0, f], z[s, 1, f], edge[s, 0, f]], axis=-1) for f in range(count)]
        for t in range(2):
            mine = jnp.concatenate([rim[t, s, pl.ds(7 * s, 8, stride=8), :], rest], axis=0).astype(BF)
            lines.append(jnp.concatenate([zc[s, t, 0], zc[s, t, 1], mine], axis=-1))
        lhs = jnp.concatenate(lines, axis=0)
        for a in range(3):
            result = mm(lhs, sw1[s, a].reshape(3 * C, 2 * C))
            for e in range(2):
                part = result[:, e * C : (e + 1) * C]
                for f in range(count):
                    base = 2 * (8 + f * tall)
                    y[s, a, e, pl.ds(base + 16, rows, stride=2), :] = part[f * rows : (f + 1) * rows]
                    for t in range(2):
                        begin = count * rows + 16 * t + 2 * f
                        y[s, a, e, pl.ds(base + 12 + t * 2 * (rows + 2), 2, stride=2), :] = part[begin : begin + 2]

    for s in range(2):
        inside = jnp.where(left if s == 0 else right, 1.0, 0.0).astype(F32)
        for e in range(2):
            state = None
            for f in range(count):
                base = 2 * (8 + f * tall)
                drive = sum(y[s, a, e, pl.ds(base + 2 * (a - 1), tall, stride=2), :] for a in range(3))
                if e == 0:
                    drive = drive * inside
                state = drive if f == 0 else decay[f : f + 1, :] * state + drive
                whole = state
                if e == 1:
                    whole = state + loc[f, pl.ds(s * (cols - 1), tall, stride=cols), :]
                ss[s, e, f] = whole
            so[s, e] = whole.astype(BF)
    late_hands[2].start()
    late_hands[0].wait_recv()
    late_hands[1].wait_recv()
    for f in range(count):
        settle(f, 0, (up, None))
        settle(f, pairs, (None, down))
    lhs = [pair_rows([s3[f, 2 * p : 2 * p + 4]], 1) for p in (0, pairs - 1) for f in range(count)]
    result = mm_halves(jnp.concatenate(lhs, axis=0), weights2[...])
    for n, p in enumerate((0, pairs - 1)):
        for f in range(count):
            finish(f, p, 1, result[(n * count + f) * cols : (n * count + f + 1) * cols])

    late_hands[2].wait_recv()
    place = lax.broadcasted_iota(jnp.int32, (tall, C), 0)
    off = jnp.logical_or(
        both(place == 7, jnp.logical_not(up)), both(place == rows + 8, jnp.logical_not(down))
    )
    for s in range(2):
        sides = []
        for f in range(count):
            pair = [
                jnp.where(off, 0.0, ss[s, e, f] + factors[f] * si[s, e].astype(F32)).astype(BF) for e in range(2)
            ]
            sides.append(jnp.concatenate(pair, axis=-1))
        lhs = jnp.concatenate(sides, axis=0)
        for a in range(3):
            result = mm(lhs, sw2[s, a].reshape(2 * C, 2 * C))
            for e in range(2):
                y2[s, a, e, pl.ds(16, count * tall, stride=2), :] = result[:, e * C : (e + 1) * C]

    for f in range(count):
        base = 2 * (8 + f * tall + 8)
        for s in range(2):
            for e in range(2):
                here = pl.ds(e if s == 0 else 7 - e, rows, stride=8)
                fix = sum(y2[s, a, e, pl.ds(base + 2 * (a - 1), rows, stride=2), :] for a in range(3))
                ot[s, f, here, :] = ot[s, f, here, :] + fix
        o[f, :, 0:8] = ot[0, f].reshape(rows, 8, C).astype(BF)
        o[f, :, cols - 8 :] = ot[1, f].reshape(rows, 8, C).astype(BF)

    for i, c in enumerate(sends):
        pl.when(around[i][1])(c.wait_send)
    for c in hands + late_hands:
        c.wait_send()


def write_out(o, out, sem):
    stores = [pltpu.make_async_copy(o.at[f], out.at[f], sem.at[f]) for f in range(o.shape[0])]
    for c in stores:
        c.start()
    for c in stores:
        c.wait()


def per_device(frames, w_in, w_out, decay, skip):
    count, _, rows, cols, _ = frames.shape
    tall = rows + 16
    spread = 2 * (count * tall + 16)
    hbm = pl.BlockSpec(memory_space=pltpu.HBM)
    vmem = pl.BlockSpec(memory_space=pltpu.VMEM)
    args = (frames[:, 0], w_in, w_out, decay, skip.reshape(1, C))
    out = pl.pallas_call(
        functools.partial(kernel, TROWS),
        out_shape=pltpu.VMEM((count, rows, cols, C), BF),
        in_specs=[hbm] * 5,
        out_specs=vmem,
        scratch_shapes=[
            pltpu.VMEM((count, rows + 4, cols, C), BF),
            pltpu.VMEM((count, rows + 4, cols, 2 * C), BF),
            pltpu.VMEM((count, rows + 2, cols, 3 * C), BF),
            pltpu.VMEM((count, tall * cols, C), F32),
            pltpu.VMEM((4 * TAPS, C, 2 * C), BF),
            pltpu.VMEM((4 * TAPS, C, 2 * C), BF),
            pltpu.VMEM((2, TAPS, 3, C, 2 * C), BF),
            pltpu.VMEM((2, TAPS, 2, C, 2 * C), BF),
            pltpu.VMEM((2, 2, count, rows, C), BF),
            pltpu.VMEM((2, 2, 2, 16, C), BF),
            pltpu.VMEM((2, 2, count, rows, C), BF),
            pltpu.VMEM((2, 2, 2, 16, C), BF),
            pltpu.VMEM((2, TAPS, 2, spread, C), F32),
            pltpu.VMEM((2, TAPS, 2, spread, C), F32),
            pltpu.VMEM((2, 2, count, tall, C), F32),
            pltpu.VMEM((2, rows * 8, C), F32),
            pltpu.VMEM((2, 2, 2, 8, C), F32),
            pltpu.VMEM((2, 2, 16 * count, C), F32),
            pltpu.VMEM((rows // 2 + 1, 2, cols, C), BF),
            pltpu.VMEM((rows // 2 + 1, 2, cols, C), BF),
            pltpu.VMEM((2, 2, tall, C), BF),
            pltpu.VMEM((2, 2, tall, C), BF),
            pltpu.VMEM((2, count, rows * 8, C), F32),
            pltpu.VMEM((count, C), F32),
            pltpu.VMEM((1, C), F32),
            pltpu.SemaphoreType.DMA((count,)),
            pltpu.SemaphoreType.DMA((28,)),
            pltpu.SemaphoreType.DMA((8,)),
            pltpu.SemaphoreType.DMA((8,)),
            pltpu.SemaphoreType.DMA((5,)),
            pltpu.SemaphoreType.DMA((5,)),
        ],
        compiler_params=pltpu.CompilerParams(
            collective_id=0, has_side_effects=True, vmem_limit_bytes=48 * 2**20
        ),
    )(*(pltpu.with_memory_space_constraint(a, pltpu.HBM) for a in args))
    out = pl.pallas_call(
        write_out,
        out_shape=jax.ShapeDtypeStruct(out.shape, BF),
        in_specs=[vmem],
        out_specs=hbm,
        scratch_shapes=[pltpu.SemaphoreType.DMA((count,))],
        compiler_params=pltpu.CompilerParams(vmem_limit_bytes=2**20),
    )(pltpu.with_memory_space_constraint(out, pltpu.VMEM))
    return out.reshape(count, 1, rows, cols, C)


def solution(mesh):
    return jax.shard_map(
        per_device,
        mesh=mesh,
        in_specs=(P("tm", "tile", None, None, None), P(), P(), P("tm", None), P()),
        out_specs=P("tm", "tile", None, None, None),
        check_vma=False,
    )
```

time: 24.2 us -> 21.3 us (0.88)
  Pallas kernels: 24.1 us -> 21.1 us
    pallas_call x1, Pallas kernels: 22.7 us -> 19.8 us  [per_device(): pl.pallas_call(functools.partial(kernel, TROWS), out_shape=pltpu.VMEM((co...]
where the time goes in v4:
time: 21.3 us; the launch traced here: 21.2 us
  Pallas kernels  21.1 us (99%)
    pallas_call x1, Pallas kernels, per_device(): pl.pallas_call(functools.partial(kernel, TROWS), out_shape=pltpu.VMEM((co...  19.8 us
    pallas_call x1, Pallas kernels, per_device(): pl.pallas_call(write_out, out_shape=jax.ShapeDtypeStruct(out.shape, BF),...  1.35 us

profile of v4, /device:TPU:1, one launch (start us, length us, event | category | flops | bytes accessed | tf_op | source)
XLA Modules:
  0.0 21.2 jit_solution(9217029346128228162)
XLA Ops:
  0.0 19.8 %shard_map.55.o = bf16[4,64,32,128]{3,2,1,0:T(8,128)(2,1)S(1)} custom-call(bf16[4,64,32,128]{3,2,1,0:T(8,128)(2,1)} %bitcast.5, bf16[3,3,128,128]{3,2,1,0:T(8,128)(2,1)} %w_in.1, bf16[3,3,128,128]{3,2,1,0:T(8,128)(2,1)} %w_out.1, f32[4,128]{1,0:T(4,128)} %decay_in.1, f32[1,128]{1,0:T(1,128)} %bitcast.6), custom_call_target="tpu_custom_call" | custom-call | tf_op jit(solution)/shard_map/pallas_call | solution.py:377
  19.8 1.3 %shard_map.56 = bf16[4,64,32,128]{3,2,1,0:T(8,128)(2,1)} custom-call(bf16[4,64,32,128]{3,2,1,0:T(8,128)(2,1)S(1)} %shard_map.55.o), custom_call_target="tpu_custom_call" | custom-call | tf_op jit(solution)/shard_map/pallas_call | solution.py:419

commit v5 on v4

--- a/solution.py
+++ b/solution.py
@@ -8,6 +8,7 @@
 from jax.sharding import PartitionSpec as P
 
 TROWS = 4
+LINE = 4
 C = 128
 BF = jnp.bfloat16
 F32 = jnp.float32
@@ -63,7 +64,7 @@
 def kernel(
     trows, frames, w_in, w_out, decay_in, skip_in, o,
     x, x3, s3, loc, pw1, pw2, sw1, sw2, edge, corner, z, zc, y, y2, ss, stage, cstage, rim, lo, inc, so, si, ot, decay, skip,
-    load_sem, w_sem, send_sem, recv_sem, tsend_sem, trecv_sem,
+    load_sem, w_sem, send_sem, recv_sem, tsend_sem, trecv_sem, far_sem,
 ):
     count, rows, cols, _ = frames.shape
     tiles = lax.axis_size("tile")
@@ -95,12 +96,16 @@
     def at(by):
         return lax.rem(me + by + tiles, tiles)
 
+    first = me == 0
+    near = [both(there, jnp.logical_not(first)) if i in (0, 4) else there for i, (_, there) in enumerate(around)]
+    to_first = {i: both(around[i][1], at(around[i][0]) == 0) for i in (1, 7)}
+
     barrier = pltpu.get_barrier_semaphore()
     greeted = jnp.int32(1)
-    for by, there in around:
-        greeted = greeted + there.astype(jnp.int32)
-
-        @pl.when(there)
+    for i, (by, there) in enumerate(around):
+        greeted = greeted + near[i].astype(jnp.int32)
+
+        @pl.when(both(there, jnp.logical_not(to_first[i])) if i in to_first else there)
         def _():
             pl.semaphore_signal(barrier, inc=1, device_id=(tm, at(by)), device_id_type=MESH)
 
@@ -180,7 +185,8 @@
     late_hands = [
         exchange(2, lo.at[pl.ds(0, 1)], inc.at[pl.ds(0, 1)]),
         exchange(3, lo.at[pl.ds(pairs, 1)], inc.at[pl.ds(pairs, 1)]),
-        exchange(4, so, si),
+        exchange(4, so.at[0], si.at[0]),
+        exchange(5, so.at[1], si.at[1]),
     ]
     weights1 = pw1.reshape(4 * TAPS * C, 2 * C)
     weights2 = pw2.reshape(4 * TAPS * C, 2 * C)
@@ -198,15 +204,21 @@
         if f == count - 1:
             lo[pl.ds(q, size)] = drive.astype(BF).reshape(size, 2, cols, C)
 
-    greet_at = jnp.where(me == 0, 1, 0)
+    spot = lax.rem(me, LINE)
+    long_way = {0: spot == 0, 1: spot == LINE - 1}
+    greet_at = jnp.where(first, 1, 0)
 
     @pl.loop(0, 2)
     def _(step):
         @pl.when(step == greet_at)
         def _():
             pl.semaphore_wait(barrier, greeted)
-            for i, c in enumerate(sends):
-                pl.when(around[i][1])(c.start)
+            for i in (1, 0, 5, 7, 4, 6, 2, 3):
+                pl.when(both(near[i], long_way[i]) if i in long_way else near[i])(sends[i].start)
+            for i, there in to_first.items():
+                @pl.when(there)
+                def _():
+                    pl.semaphore_signal(far_sem, inc=1, device_id=(tm, at(around[i][0])), device_id_type=MESH)
 
         @pl.when(step != greet_at)
         def _():
@@ -224,6 +236,8 @@
 
     pl.when(greet_at == 1)(hands[0].start)
     hands[1].start()
+    for i, far in long_way.items():
+        pl.when(both(near[i], jnp.logical_not(far)))(sends[i].start)
 
     factors = []
     for f in range(count):
@@ -257,6 +271,13 @@
     inner = [(1, half - 1), (half, half - 1)]
     for n, (q, size) in enumerate(chunks):
         hands[n].wait_recv()
+        if n == 1:
+            @pl.when(first)
+            def _():
+                pl.semaphore_wait(far_sem, 2)
+                sends[0].start()
+                sends[4].start()
+
         p, deep = inner[n]
         for f in range(count):
             for i in range(q, q + size):
@@ -266,22 +287,12 @@
 
     for c in placed[then_needed:]:
         c.wait()
-    for i, c in enumerate(sends):
-        pl.when(comes[i])(c.wait_recv)
-    for f in range(count):
-        for t in range(2):
-            wide = widen(f, t * (rows + 2), 2)
-            rim[t, 0, 16 * f : 16 * f + 16] = wide[:, :8].reshape(16, C)
-            rim[t, 1, 16 * f : 16 * f + 16] = wide[:, cols - 8 :].reshape(16, C)
-    lhs = [pair_rows(frame_rows(f, pl.ds(2 * q, 4)), 1) for q in (0, pairs) for f in range(count)]
-    drive = mm_halves(jnp.concatenate(lhs, axis=0), weights1[...])
-    for n, q in enumerate((0, pairs)):
-        for f in range(count):
-            recur(f, q, 1, drive[(n * count + f) * cols : (n * count + f + 1) * cols])
-    late_hands[0].start()
-    late_hands[1].start()
-
-    for s in range(2):
+
+    def arrive(*which):
+        for i in which:
+            pl.when(comes[i])(sends[i].wait_recv)
+
+    def side_in(s):
         lines = [jnp.concatenate([z[s, 0, f], z[s, 1, f], edge[s, 0, f]], axis=-1) for f in range(count)]
         for t in range(2):
             mine = jnp.concatenate([rim[t, s, pl.ds(7 * s, 8, stride=8), :], rest], axis=0).astype(BF)
@@ -298,7 +309,6 @@
                         begin = count * rows + 16 * t + 2 * f
                         y[s, a, e, pl.ds(base + 12 + t * 2 * (rows + 2), 2, stride=2), :] = part[begin : begin + 2]
 
-    for s in range(2):
         inside = jnp.where(left if s == 0 else right, 1.0, 0.0).astype(F32)
         for e in range(2):
             state = None
@@ -313,24 +323,15 @@
                     whole = state + loc[f, pl.ds(s * (cols - 1), tall, stride=cols), :]
                 ss[s, e, f] = whole
             so[s, e] = whole.astype(BF)
-    late_hands[2].start()
-    late_hands[0].wait_recv()
-    late_hands[1].wait_recv()
-    for f in range(count):
-        settle(f, 0, (up, None))
-        settle(f, pairs, (None, down))
-    lhs = [pair_rows([s3[f, 2 * p : 2 * p + 4]], 1) for p in (0, pairs - 1) for f in range(count)]
-    result = mm_halves(jnp.concatenate(lhs, axis=0), weights2[...])
-    for n, p in enumerate((0, pairs - 1)):
-        for f in range(count):
-            finish(f, p, 1, result[(n * count + f) * cols : (n * count + f + 1) * cols])
-
-    late_hands[2].wait_recv()
+        late_hands[2 + s].start()
+
     place = lax.broadcasted_iota(jnp.int32, (tall, C), 0)
     off = jnp.logical_or(
         both(place == 7, jnp.logical_not(up)), both(place == rows + 8, jnp.logical_not(down))
     )
-    for s in range(2):
+
+    def side_out(s):
+        late_hands[2 + s].wait_recv()
         sides = []
         for f in range(count):
             pair = [
@@ -342,16 +343,47 @@
             result = mm(lhs, sw2[s, a].reshape(2 * C, 2 * C))
             for e in range(2):
                 y2[s, a, e, pl.ds(16, count * tall, stride=2), :] = result[:, e * C : (e + 1) * C]
-
-    for f in range(count):
-        base = 2 * (8 + f * tall + 8)
-        for s in range(2):
+        for f in range(count):
+            base = 2 * (8 + f * tall + 8)
             for e in range(2):
                 here = pl.ds(e if s == 0 else 7 - e, rows, stride=8)
                 fix = sum(y2[s, a, e, pl.ds(base + 2 * (a - 1), rows, stride=2), :] for a in range(3))
                 ot[s, f, here, :] = ot[s, f, here, :] + fix
-        o[f, :, 0:8] = ot[0, f].reshape(rows, 8, C).astype(BF)
-        o[f, :, cols - 8 :] = ot[1, f].reshape(rows, 8, C).astype(BF)
+            begin = s * (cols - 8)
+            o[f, :, begin : begin + 8] = ot[s, f].reshape(rows, 8, C).astype(BF)
+
+    arrive(2, 3)
+    for f in range(count):
+        for t in range(2):
+            wide = widen(f, t * (rows + 2), 2)
+            rim[t, 0, 16 * f : 16 * f + 16] = wide[:, :8].reshape(16, C)
+            rim[t, 1, 16 * f : 16 * f + 16] = wide[:, cols - 8 :].reshape(16, C)
+    lhs = [pair_rows(frame_rows(f, pl.ds(2 * q, 4)), 1) for q in (0, pairs) for f in range(count)]
+    drive = mm_halves(jnp.concatenate(lhs, axis=0), weights1[...])
+    for n, q in enumerate((0, pairs)):
+        for f in range(count):
+            recur(f, q, 1, drive[(n * count + f) * cols : (n * count + f + 1) * cols])
+    late_hands[0].start()
+    late_hands[1].start()
+
+    arrive(0, 4, 6)
+    side_in(1)
+
+    late_hands[0].wait_recv()
+    late_hands[1].wait_recv()
+    for f in range(count):
+        settle(f, 0, (up, None))
+        settle(f, pairs, (None, down))
+    lhs = [pair_rows([s3[f, 2 * p : 2 * p + 4]], 1) for p in (0, pairs - 1) for f in range(count)]
+    result = mm_halves(jnp.concatenate(lhs, axis=0), weights2[...])
+    for n, p in enumerate((0, pairs - 1)):
+        for f in range(count):
+            finish(f, p, 1, result[(n * count + f) * cols : (n * count + f + 1) * cols])
+
+    arrive(1, 5, 7)
+    side_in(0)
+    side_out(1)
+    side_out(0)
 
     for i, c in enumerate(sends):
         pl.when(around[i][1])(c.wait_send)
@@ -409,8 +441,9 @@
             pltpu.SemaphoreType.DMA((28,)),
             pltpu.SemaphoreType.DMA((8,)),
             pltpu.SemaphoreType.DMA((8,)),
-            pltpu.SemaphoreType.DMA((5,)),
-            pltpu.SemaphoreType.DMA((5,)),
+            pltpu.SemaphoreType.DMA((6,)),
+            pltpu.SemaphoreType.DMA((6,)),
+            pltpu.SemaphoreType.REGULAR,
         ],
         compiler_params=pltpu.CompilerParams(
             collective_id=0, has_side_effects=True, vmem_limit_bytes=48 * 2**20

time: 21.3 us -> 22 us (1.033)
  Pallas kernels: 21.1 us -> 21.9 us
    pallas_call x1, Pallas kernels: 19.8 us -> 20.5 us  [per_device(): pl.pallas_call(functools.partial(kernel, TROWS), out_shape=pltpu.VMEM((co...]
where the time goes in v5:
time: 22 us; the launch traced here: 21.9 us
  Pallas kernels  21.9 us (100%)
    pallas_call x1, Pallas kernels, per_device(): pl.pallas_call(functools.partial(kernel, TROWS), out_shape=pltpu.VMEM((co...  20.5 us
    pallas_call x1, Pallas kernels, per_device(): pl.pallas_call(write_out, out_shape=jax.ShapeDtypeStruct(out.shape, BF),...  1.35 us

profile of v5, /device:TPU:1, one launch (start us, length us, event | category | flops | bytes accessed | tf_op | source)
XLA Modules:
  0.0 21.9 jit_solution(6591244823509570925)
XLA Ops:
  0.0 20.5 %shard_map.55.o = bf16[4,64,32,128]{3,2,1,0:T(8,128)(2,1)S(1)} custom-call(bf16[4,64,32,128]{3,2,1,0:T(8,128)(2,1)} %bitcast.5, bf16[3,3,128,128]{3,2,1,0:T(8,128)(2,1)} %w_in.1, bf16[3,3,128,128]{3,2,1,0:T(8,128)(2,1)} %w_out.1, f32[4,128]{1,0:T(4,128)} %decay_in.1, f32[1,128]{1,0:T(1,128)} %bitcast.6), custom_call_target="tpu_custom_call" | custom-call | tf_op jit(solution)/shard_map/pallas_call | solution.py:409
  20.5 1.3 %shard_map.56 = bf16[4,64,32,128]{3,2,1,0:T(8,128)(2,1)} custom-call(bf16[4,64,32,128]{3,2,1,0:T(8,128)(2,1)S(1)} %shard_map.55.o), custom_call_target="tpu_custom_call" | custom-call | tf_op jit(solution)/shard_map/pallas_call | solution.py:452

commit v6 on v4

--- a/solution.py
+++ b/solution.py
@@ -8,6 +8,7 @@
 from jax.sharding import PartitionSpec as P
 
 TROWS = 4
+LINE = 4
 C = 128
 BF = jnp.bfloat16
 F32 = jnp.float32
@@ -63,7 +64,7 @@
 def kernel(
     trows, frames, w_in, w_out, decay_in, skip_in, o,
     x, x3, s3, loc, pw1, pw2, sw1, sw2, edge, corner, z, zc, y, y2, ss, stage, cstage, rim, lo, inc, so, si, ot, decay, skip,
-    load_sem, w_sem, send_sem, recv_sem, tsend_sem, trecv_sem,
+    load_sem, w_sem, send_sem, recv_sem, tsend_sem, trecv_sem, far_sem,
 ):
     count, rows, cols, _ = frames.shape
     tiles = lax.axis_size("tile")
@@ -95,12 +96,17 @@
     def at(by):
         return lax.rem(me + by + tiles, tiles)
 
+    first = me == 0
+    near = [both(there, jnp.logical_not(first)) for _, there in around]
+    to_first = [both(there, at(by) == 0) for by, there in around]
+
     barrier = pltpu.get_barrier_semaphore()
-    greeted = jnp.int32(1)
-    for by, there in around:
-        greeted = greeted + there.astype(jnp.int32)
-
-        @pl.when(there)
+    greeted, far = jnp.int32(1), jnp.int32(0)
+    for i, (by, there) in enumerate(around):
+        greeted = greeted + near[i].astype(jnp.int32)
+        far = far + both(there, first).astype(jnp.int32)
+
+        @pl.when(both(there, jnp.logical_not(to_first[i])))
         def _():
             pl.semaphore_signal(barrier, inc=1, device_id=(tm, at(by)), device_id_type=MESH)
 
@@ -198,31 +204,37 @@
         if f == count - 1:
             lo[pl.ds(q, size)] = drive.astype(BF).reshape(size, 2, cols, C)
 
-    greet_at = jnp.where(me == 0, 1, 0)
+    def first_conv(n):
+        q, size = chunks[n]
+        for f in range(count):
+            end = rows + 2 if n else 2 * half + 4
+            for start in range(2 + n * (2 * half + 2), end, 2):
+                widen(f, start, 2)
+            lhs = pair_rows(frame_rows(f, pl.ds(2 * q, 2 * size + 2)), size)
+            recur(f, q, size, mm(lhs, weights1[...]))
+
+    greet_at = jnp.where(lax.rem(me, LINE) == 0, 1, 0)
 
     @pl.loop(0, 2)
     def _(step):
         @pl.when(step == greet_at)
         def _():
             pl.semaphore_wait(barrier, greeted)
-            for i, c in enumerate(sends):
-                pl.when(around[i][1])(c.start)
+            for i in (1, 0, 5, 7, 4, 6, 2, 3):
+                pl.when(near[i])(sends[i].start)
+            for i, (by, _) in enumerate(around):
+                @pl.when(to_first[i])
+                def _():
+                    pl.semaphore_signal(far_sem, inc=1, device_id=(tm, at(by)), device_id_type=MESH)
 
         @pl.when(step != greet_at)
         def _():
             for c in placed[:first_needed]:
                 c.wait()
-            for n, (q, size) in enumerate(chunks):
-                for f in range(count):
-                    end = rows + 2 if n else 2 * half + 4
-                    for start in range(2 + n * (2 * half + 2), end, 2):
-                        widen(f, start, 2)
-                    lhs = pair_rows(frame_rows(f, pl.ds(2 * q, 2 * size + 2)), size)
-                    recur(f, q, size, mm(lhs, weights1[...]))
-                if n == 0:
-                    pl.when(greet_at == 0)(hands[0].start)
-
-    pl.when(greet_at == 1)(hands[0].start)
+            first_conv(0)
+
+    hands[0].start()
+    first_conv(1)
     hands[1].start()
 
     factors = []
@@ -255,65 +267,85 @@
     for c in placed[first_needed:then_needed]:
         c.wait()
     inner = [(1, half - 1), (half, half - 1)]
-    for n, (q, size) in enumerate(chunks):
+
+    def second_conv(n):
+        q, size = chunks[n]
+        p, deep = inner[n]
         hands[n].wait_recv()
-        p, deep = inner[n]
         for f in range(count):
             for i in range(q, q + size):
                 settle(f, i)
             lhs = pair_rows([s3[f, 2 * p : 2 * p + 2 * deep + 2]], deep)
             finish(f, p, deep, mm(lhs, weights2[...]))
 
-    for c in placed[then_needed:]:
-        c.wait()
-    for i, c in enumerate(sends):
-        pl.when(comes[i])(c.wait_recv)
-    for f in range(count):
-        for t in range(2):
-            wide = widen(f, t * (rows + 2), 2)
-            rim[t, 0, 16 * f : 16 * f + 16] = wide[:, :8].reshape(16, C)
-            rim[t, 1, 16 * f : 16 * f + 16] = wide[:, cols - 8 :].reshape(16, C)
-    lhs = [pair_rows(frame_rows(f, pl.ds(2 * q, 4)), 1) for q in (0, pairs) for f in range(count)]
-    drive = mm_halves(jnp.concatenate(lhs, axis=0), weights1[...])
-    for n, q in enumerate((0, pairs)):
-        for f in range(count):
-            recur(f, q, 1, drive[(n * count + f) * cols : (n * count + f + 1) * cols])
-    late_hands[0].start()
-    late_hands[1].start()
-
-    for s in range(2):
-        lines = [jnp.concatenate([z[s, 0, f], z[s, 1, f], edge[s, 0, f]], axis=-1) for f in range(count)]
-        for t in range(2):
-            mine = jnp.concatenate([rim[t, s, pl.ds(7 * s, 8, stride=8), :], rest], axis=0).astype(BF)
-            lines.append(jnp.concatenate([zc[s, t, 0], zc[s, t, 1], mine], axis=-1))
-        lhs = jnp.concatenate(lines, axis=0)
-        for a in range(3):
-            result = mm(lhs, sw1[s, a].reshape(3 * C, 2 * C))
-            for e in range(2):
-                part = result[:, e * C : (e + 1) * C]
+    second_conv(0)
+
+    @pl.when(first)
+    def _():
+        pl.semaphore_wait(far_sem, far)
+        for i, c in enumerate(sends):
+            pl.when(around[i][1])(c.start)
+
+    late_at = jnp.where(first, 1, 0)
+
+    @pl.loop(0, 2)
+    def _(step):
+        @pl.when(step != late_at)
+        def _():
+            second_conv(1)
+
+        @pl.when(step == late_at)
+        def _():
+            for c in placed[then_needed:]:
+                c.wait()
+            for i, c in enumerate(sends):
+                pl.when(comes[i])(c.wait_recv)
+            for f in range(count):
+                for t in range(2):
+                    wide = widen(f, t * (rows + 2), 2)
+                    rim[t, 0, 16 * f : 16 * f + 16] = wide[:, :8].reshape(16, C)
+                    rim[t, 1, 16 * f : 16 * f + 16] = wide[:, cols - 8 :].reshape(16, C)
+            lhs = [pair_rows(frame_rows(f, pl.ds(2 * q, 4)), 1) for q in (0, pairs) for f in range(count)]
+            drive = mm_halves(jnp.concatenate(lhs, axis=0), weights1[...])
+            for n, q in enumerate((0, pairs)):
                 for f in range(count):
-                    base = 2 * (8 + f * tall)
-                    y[s, a, e, pl.ds(base + 16, rows, stride=2), :] = part[f * rows : (f + 1) * rows]
-                    for t in range(2):
-                        begin = count * rows + 16 * t + 2 * f
-                        y[s, a, e, pl.ds(base + 12 + t * 2 * (rows + 2), 2, stride=2), :] = part[begin : begin + 2]
-
-    for s in range(2):
-        inside = jnp.where(left if s == 0 else right, 1.0, 0.0).astype(F32)
-        for e in range(2):
-            state = None
-            for f in range(count):
-                base = 2 * (8 + f * tall)
-                drive = sum(y[s, a, e, pl.ds(base + 2 * (a - 1), tall, stride=2), :] for a in range(3))
-                if e == 0:
-                    drive = drive * inside
-                state = drive if f == 0 else decay[f : f + 1, :] * state + drive
-                whole = state
-                if e == 1:
-                    whole = state + loc[f, pl.ds(s * (cols - 1), tall, stride=cols), :]
-                ss[s, e, f] = whole
-            so[s, e] = whole.astype(BF)
-    late_hands[2].start()
+                    recur(f, q, 1, drive[(n * count + f) * cols : (n * count + f + 1) * cols])
+            late_hands[0].start()
+            late_hands[1].start()
+
+            for s in range(2):
+                lines = [jnp.concatenate([z[s, 0, f], z[s, 1, f], edge[s, 0, f]], axis=-1) for f in range(count)]
+                for t in range(2):
+                    mine = jnp.concatenate([rim[t, s, pl.ds(7 * s, 8, stride=8), :], rest], axis=0).astype(BF)
+                    lines.append(jnp.concatenate([zc[s, t, 0], zc[s, t, 1], mine], axis=-1))
+                lhs = jnp.concatenate(lines, axis=0)
+                for a in range(3):
+                    result = mm(lhs, sw1[s, a].reshape(3 * C, 2 * C))
+                    for e in range(2):
+                        part = result[:, e * C : (e + 1) * C]
+                        for f in range(count):
+                            base = 2 * (8 + f * tall)
+                            y[s, a, e, pl.ds(base + 16, rows, stride=2), :] = part[f * rows : (f + 1) * rows]
+                            for t in range(2):
+                                begin = count * rows + 16 * t + 2 * f
+                                y[s, a, e, pl.ds(base + 12 + t * 2 * (rows + 2), 2, stride=2), :] = part[begin : begin + 2]
+
+            for s in range(2):
+                inside = jnp.where(left if s == 0 else right, 1.0, 0.0).astype(F32)
+                for e in range(2):
+                    state = None
+                    for f in range(count):
+                        base = 2 * (8 + f * tall)
+                        drive = sum(y[s, a, e, pl.ds(base + 2 * (a - 1), tall, stride=2), :] for a in range(3))
+                        if e == 0:
+                            drive = drive * inside
+                        state = drive if f == 0 else decay[f : f + 1, :] * state + drive
+                        whole = state
+                        if e == 1:
+                            whole = state + loc[f, pl.ds(s * (cols - 1), tall, stride=cols), :]
+                        ss[s, e, f] = whole
+                    so[s, e] = whole.astype(BF)
+            late_hands[2].start()
     late_hands[0].wait_recv()
     late_hands[1].wait_recv()
     for f in range(count):
@@ -411,6 +443,7 @@
             pltpu.SemaphoreType.DMA((8,)),
             pltpu.SemaphoreType.DMA((5,)),
             pltpu.SemaphoreType.DMA((5,)),
+            pltpu.SemaphoreType.REGULAR,
         ],
         compiler_params=pltpu.CompilerParams(
             collective_id=0, has_side_effects=True, vmem_limit_bytes=48 * 2**20

time: 21.3 us -> 21.4 us (level)
  no operation moved by 1% of the time
where the time goes in v6:
time: 21.4 us; the launch traced here: 21.3 us
  Pallas kernels  21.3 us (100%)
    pallas_call x1, Pallas kernels, per_device(): pl.pallas_call(functools.partial(kernel, TROWS), out_shape=pltpu.VMEM((co...  19.9 us
    pallas_call x1, Pallas kernels, per_device(): pl.pallas_call(write_out, out_shape=jax.ShapeDtypeStruct(out.shape, BF),...  1.35 us

profile of v6, /device:TPU:1, one launch (start us, length us, event | category | flops | bytes accessed | tf_op | source)
XLA Modules:
  0.0 21.3 jit_solution(641452224729845270)
XLA Ops:
  0.0 19.9 %shard_map.55.o = bf16[4,64,32,128]{3,2,1,0:T(8,128)(2,1)S(1)} custom-call(bf16[4,64,32,128]{3,2,1,0:T(8,128)(2,1)} %bitcast.5, bf16[3,3,128,128]{3,2,1,0:T(8,128)(2,1)} %w_in.1, bf16[3,3,128,128]{3,2,1,0:T(8,128)(2,1)} %w_out.1, f32[4,128]{1,0:T(4,128)} %decay_in.1, f32[1,128]{1,0:T(1,128)} %bitcast.6), custom_call_target="tpu_custom_call" | custom-call | tf_op jit(solution)/shard_map/pallas_call | solution.py:409
  19.9 1.3 %shard_map.56 = bf16[4,64,32,128]{3,2,1,0:T(8,128)(2,1)} custom-call(bf16[4,64,32,128]{3,2,1,0:T(8,128)(2,1)S(1)} %shard_map.55.o), custom_call_target="tpu_custom_call" | custom-call | tf_op jit(solution)/shard_map/pallas_call | solution.py:452

commit v7 on v6

--- a/solution.py
+++ b/solution.py
@@ -26,25 +26,32 @@
     return mm(lhs[:, :half], rhs[:half]) + mm(lhs[:, half:], rhs[half:])
 
 
-def pair_weights(w, pair):
+def pair_zeros(pair):
     zero = jnp.zeros((TAPS, C, C), BF)
     pair[3 * TAPS : 4 * TAPS, :, 0:C] = zero
     pair[0:TAPS, :, C : 2 * C] = zero
+
+
+def pair_copies(w, pair):
     return [
         (w.at[i], pair.at[pl.ds((i + e) * TAPS, TAPS), :, pl.ds(e * C, C)]) for i in range(TAPS) for e in range(2)
     ]
 
 
-def side_weights(w, side, table):
-    copies = []
-    for s in range(2):
-        for k, taps in enumerate(table[s]):
-            for e, b in enumerate(taps):
-                if b is None:
-                    side[s, :, k, :, e * C : (e + 1) * C] = jnp.zeros((TAPS, C, C), BF)
-                else:
-                    copies.append((w.at[:, b], side.at[s, :, k, :, pl.ds(e * C, C)]))
-    return copies
+def side_blocks(table):
+    return [(s, k, e, b) for s in range(2) for k, taps in enumerate(table[s]) for e, b in enumerate(taps)]
+
+
+def side_zeros(side, table):
+    for s, k, e, b in side_blocks(table):
+        if b is None:
+            side[s, :, k, :, e * C : (e + 1) * C] = jnp.zeros((TAPS, C, C), BF)
+
+
+def side_copies(w, side, table):
+    return [
+        (w.at[:, b], side.at[s, :, k, :, pl.ds(e * C, C)]) for s, k, e, b in side_blocks(table) if b is not None
+    ]
 
 
 SIDE_IN = (((1, 0), (0, None), (2, None)), ((1, 2), (2, None), (0, None)))
@@ -112,14 +119,24 @@
 
     pl.semaphore_signal(barrier, inc=1, device_id=(1 - tm, me), device_id_type=MESH)
 
-    placed = pair_weights(w_in, pw1) + [(decay_in, decay), (skip_in, skip)]
+    placed = pair_copies(w_in, pw1) + [(decay_in, decay), (skip_in, skip)]
     first_needed = len(placed)
-    placed += pair_weights(w_out, pw2)
+    placed += pair_copies(w_out, pw2)
     then_needed = len(placed)
-    placed += side_weights(w_in, sw1, SIDE_IN) + side_weights(w_out, sw2, SIDE_OUT)
+    placed += side_copies(w_in, sw1, SIDE_IN) + side_copies(w_out, sw2, SIDE_OUT)
     placed = [pltpu.make_async_copy(src, dst, w_sem.at[i]) for i, (src, dst) in enumerate(placed)]
-    for c in placed:
+    for c in placed[:first_needed]:
         c.start()
+
+    def greet():
+        pl.semaphore_wait(barrier, greeted)
+        for i, (by, _) in enumerate(around):
+            @pl.when(to_first[i])
+            def _():
+                pl.semaphore_signal(far_sem, inc=1, device_id=(tm, at(by)), device_id_type=MESH)
+
+    starts_line = lax.rem(me, LINE) == 0
+    pl.when(jnp.logical_not(starts_line))(greet)
 
     for f in range(count):
         loads[f].wait()
@@ -156,11 +173,6 @@
         for i, (src, dst) in enumerate(plan)
     ]
     comes = [around[i ^ 1][1] if i < 4 else around[11 - i][1] for i in range(8)]
-    for i, (_, dst) in enumerate(plan):
-        @pl.when(jnp.logical_not(comes[i]))
-        def _():
-            dst[...] = jnp.zeros(dst.shape, BF)
-
     in_tile = lax.broadcasted_iota(jnp.int32, (1, 8, C), 1)
 
     def widen(f, start, size):
@@ -213,22 +225,21 @@
             lhs = pair_rows(frame_rows(f, pl.ds(2 * q, 2 * size + 2)), size)
             recur(f, q, size, mm(lhs, weights1[...]))
 
-    greet_at = jnp.where(lax.rem(me, LINE) == 0, 1, 0)
+    greet_at = jnp.where(starts_line, 1, 0)
 
     @pl.loop(0, 2)
     def _(step):
         @pl.when(step == greet_at)
         def _():
-            pl.semaphore_wait(barrier, greeted)
+            pl.when(starts_line)(greet)
             for i in (1, 0, 5, 7, 4, 6, 2, 3):
                 pl.when(near[i])(sends[i].start)
-            for i, (by, _) in enumerate(around):
-                @pl.when(to_first[i])
-                def _():
-                    pl.semaphore_signal(far_sem, inc=1, device_id=(tm, at(by)), device_id_type=MESH)
 
         @pl.when(step != greet_at)
         def _():
+            for c in placed[first_needed:]:
+                c.start()
+            pair_zeros(pw1)
             for c in placed[:first_needed]:
                 c.wait()
             first_conv(0)
@@ -264,21 +275,31 @@
         ot[1, f, pl.ds(16 * p, 16 * size)] = mixed[:, cols - 8 :].reshape(16 * size, C)
         o[f, pl.ds(2 * p, 2 * size), 8 : cols - 8] = mixed[:, 8 : cols - 8].astype(BF)
 
+    pair_zeros(pw2)
+    side_zeros(sw1, SIDE_IN)
+    side_zeros(sw2, SIDE_OUT)
+    for i, (_, dst) in enumerate(plan):
+        @pl.when(jnp.logical_not(comes[i]))
+        def _():
+            dst[...] = jnp.zeros(dst.shape, BF)
+
     for c in placed[first_needed:then_needed]:
         c.wait()
     inner = [(1, half - 1), (half, half - 1)]
 
-    def second_conv(n):
+    def second_conv(n, which):
         q, size = chunks[n]
         p, deep = inner[n]
-        hands[n].wait_recv()
-        for f in range(count):
+        for f in which:
             for i in range(q, q + size):
                 settle(f, i)
             lhs = pair_rows([s3[f, 2 * p : 2 * p + 2 * deep + 2]], deep)
             finish(f, p, deep, mm(lhs, weights2[...]))
 
-    second_conv(0)
+    hands[0].wait_recv()
+    second_conv(0, range(count))
+    hands[1].wait_recv()
+    second_conv(1, range(count // 2))
 
     @pl.when(first)
     def _():
@@ -286,33 +307,33 @@
         for i, c in enumerate(sends):
             pl.when(around[i][1])(c.start)
 
-    late_at = jnp.where(first, 1, 0)
+    def arrive(*which):
+        for i in which:
+            pl.when(comes[i])(sends[i].wait_recv)
+
+    arrive(2, 3)
+    for f in range(count):
+        for t in range(2):
+            wide = widen(f, t * (rows + 2), 2)
+            rim[t, 0, 16 * f : 16 * f + 16] = wide[:, :8].reshape(16, C)
+            rim[t, 1, 16 * f : 16 * f + 16] = wide[:, cols - 8 :].reshape(16, C)
+    lhs = [pair_rows(frame_rows(f, pl.ds(2 * q, 4)), 1) for q in (0, pairs) for f in range(count)]
+    drive = mm_halves(jnp.concatenate(lhs, axis=0), weights1[...])
+    for n, q in enumerate((0, pairs)):
+        for f in range(count):
+            recur(f, q, 1, drive[(n * count + f) * cols : (n * count + f + 1) * cols])
+    late_hands[0].start()
+    late_hands[1].start()
+
+    sides_at = jnp.where(first, 1, 0)
 
     @pl.loop(0, 2)
     def _(step):
-        @pl.when(step != late_at)
-        def _():
-            second_conv(1)
-
-        @pl.when(step == late_at)
+        @pl.when(step == sides_at)
         def _():
             for c in placed[then_needed:]:
                 c.wait()
-            for i, c in enumerate(sends):
-                pl.when(comes[i])(c.wait_recv)
-            for f in range(count):
-                for t in range(2):
-                    wide = widen(f, t * (rows + 2), 2)
-                    rim[t, 0, 16 * f : 16 * f + 16] = wide[:, :8].reshape(16, C)
-                    rim[t, 1, 16 * f : 16 * f + 16] = wide[:, cols - 8 :].reshape(16, C)
-            lhs = [pair_rows(frame_rows(f, pl.ds(2 * q, 4)), 1) for q in (0, pairs) for f in range(count)]
-            drive = mm_halves(jnp.concatenate(lhs, axis=0), weights1[...])
-            for n, q in enumerate((0, pairs)):
-                for f in range(count):
-                    recur(f, q, 1, drive[(n * count + f) * cols : (n * count + f + 1) * cols])
-            late_hands[0].start()
-            late_hands[1].start()
-
+            arrive(0, 4, 6, 1, 5, 7)
             for s in range(2):
                 lines = [jnp.concatenate([z[s, 0, f], z[s, 1, f], edge[s, 0, f]], axis=-1) for f in range(count)]
                 for t in range(2):
@@ -346,16 +367,20 @@
                         ss[s, e, f] = whole
                     so[s, e] = whole.astype(BF)
             late_hands[2].start()
-    late_hands[0].wait_recv()
-    late_hands[1].wait_recv()
-    for f in range(count):
-        settle(f, 0, (up, None))
-        settle(f, pairs, (None, down))
-    lhs = [pair_rows([s3[f, 2 * p : 2 * p + 4]], 1) for p in (0, pairs - 1) for f in range(count)]
-    result = mm_halves(jnp.concatenate(lhs, axis=0), weights2[...])
-    for n, p in enumerate((0, pairs - 1)):
-        for f in range(count):
-            finish(f, p, 1, result[(n * count + f) * cols : (n * count + f + 1) * cols])
+
+        @pl.when(step != sides_at)
+        def _():
+            second_conv(1, range(count // 2, count))
+            late_hands[0].wait_recv()
+            late_hands[1].wait_recv()
+            for f in range(count):
+                settle(f, 0, (up, None))
+                settle(f, pairs, (None, down))
+            lhs = [pair_rows([s3[f, 2 * p : 2 * p + 4]], 1) for p in (0, pairs - 1) for f in range(count)]
+            result = mm_halves(jnp.concatenate(lhs, axis=0), weights2[...])
+            for n, p in enumerate((0, pairs - 1)):
+                for f in range(count):
+                    finish(f, p, 1, result[(n * count + f) * cols : (n * count + f + 1) * cols])
 
     late_hands[2].wait_recv()
     place = lax.broadcasted_iota(jnp.int32, (tall, C), 0)

time: 21.4 us -> 22.8 us (1.065)
  Pallas kernels: 21.3 us -> 22.7 us
    pallas_call x1, Pallas kernels: 19.9 us -> 21.3 us  [per_device(): pl.pallas_call(functools.partial(kernel, TROWS), out_shape=pltpu.VMEM((co...]
where the time goes in v7:
time: 22.8 us; the launch traced here: 22.7 us
  Pallas kernels  22.7 us (100%)
    pallas_call x1, Pallas kernels, per_device(): pl.pallas_call(functools.partial(kernel, TROWS), out_shape=pltpu.VMEM((co...  21.3 us
    pallas_call x1, Pallas kernels, per_device(): pl.pallas_call(write_out, out_shape=jax.ShapeDtypeStruct(out.shape, BF),...  1.35 us

profile of v7, /device:TPU:1, one launch (start us, length us, event | category | flops | bytes accessed | tf_op | source)
XLA Modules:
  0.0 22.7 jit_solution(5363565172623029901)
XLA Ops:
  0.0 21.3 %shard_map.55.o = bf16[4,64,32,128]{3,2,1,0:T(8,128)(2,1)S(1)} custom-call(bf16[4,64,32,128]{3,2,1,0:T(8,128)(2,1)} %bitcast.5, bf16[3,3,128,128]{3,2,1,0:T(8,128)(2,1)} %w_in.1, bf16[3,3,128,128]{3,2,1,0:T(8,128)(2,1)} %w_out.1, f32[4,128]{1,0:T(4,128)} %decay_in.1, f32[1,128]{1,0:T(1,128)} %bitcast.6), custom_call_target="tpu_custom_call" | custom-call | tf_op jit(solution)/shard_map/pallas_call | solution.py:434
  21.4 1.3 %shard_map.56 = bf16[4,64,32,128]{3,2,1,0:T(8,128)(2,1)} custom-call(bf16[4,64,32,128]{3,2,1,0:T(8,128)(2,1)S(1)} %shard_map.55.o), custom_call_target="tpu_custom_call" | custom-call | tf_op jit(solution)/shard_map/pallas_call | solution.py:477

commit v8 on v7

--- a/solution.py
+++ b/solution.py
@@ -108,10 +108,9 @@
     to_first = [both(there, at(by) == 0) for by, there in around]
 
     barrier = pltpu.get_barrier_semaphore()
-    greeted, far = jnp.int32(1), jnp.int32(0)
+    greeted = jnp.int32(1)
     for i, (by, there) in enumerate(around):
         greeted = greeted + near[i].astype(jnp.int32)
-        far = far + both(there, first).astype(jnp.int32)
 
         @pl.when(both(there, jnp.logical_not(to_first[i])))
         def _():
@@ -133,7 +132,7 @@
         for i, (by, _) in enumerate(around):
             @pl.when(to_first[i])
             def _():
-                pl.semaphore_signal(far_sem, inc=1, device_id=(tm, at(by)), device_id_type=MESH)
+                pl.semaphore_signal(far_sem.at[i], inc=1, device_id=(tm, at(by)), device_id_type=MESH)
 
     starts_line = lax.rem(me, LINE) == 0
     pl.when(jnp.logical_not(starts_line))(greet)
@@ -232,7 +231,7 @@
         @pl.when(step == greet_at)
         def _():
             pl.when(starts_line)(greet)
-            for i in (1, 0, 5, 7, 4, 6, 2, 3):
+            for i in (1, 5, 7, 4, 6, 3):
                 pl.when(near[i])(sends[i].start)
 
         @pl.when(step != greet_at)
@@ -245,6 +244,8 @@
             first_conv(0)
 
     hands[0].start()
+    for i in (0, 2):
+        pl.when(near[i])(sends[i].start)
     first_conv(1)
     hands[1].start()
 
@@ -303,9 +304,11 @@
 
     @pl.when(first)
     def _():
-        pl.semaphore_wait(far_sem, far)
-        for i, c in enumerate(sends):
-            pl.when(around[i][1])(c.start)
+        for i, opposite in ((2, 3), (3, 2), (4, 7), (5, 6), (6, 5), (7, 4), (0, 1), (1, 0)):
+            @pl.when(around[i][1])
+            def _():
+                pl.semaphore_wait(far_sem.at[opposite], 1)
+                sends[i].start()
 
     def arrive(*which):
         for i in which:
@@ -468,7 +471,7 @@
             pltpu.SemaphoreType.DMA((8,)),
             pltpu.SemaphoreType.DMA((5,)),
             pltpu.SemaphoreType.DMA((5,)),
-            pltpu.SemaphoreType.REGULAR,
+            pltpu.SemaphoreType.REGULAR((8,)),
         ],
         compiler_params=pltpu.CompilerParams(
             collective_id=0, has_side_effects=True, vmem_limit_bytes=48 * 2**20

time: 22.8 us -> 22.9 us (level)
  no operation moved by 1% of the time
where the time goes in v8:
time: 22.9 us; the launch traced here: 22.8 us
  Pallas kernels  22.7 us (99%)
    pallas_call x1, Pallas kernels, per_device(): pl.pallas_call(functools.partial(kernel, TROWS), out_shape=pltpu.VMEM((co...  21.4 us
    pallas_call x1, Pallas kernels, per_device(): pl.pallas_call(write_out, out_shape=jax.ShapeDtypeStruct(out.shape, BF),...  1.35 us

profile of v8, /device:TPU:1, one launch (start us, length us, event | category | flops | bytes accessed | tf_op | source)
XLA Modules:
  0.0 22.8 jit_solution(17755494736717953933)
XLA Ops:
  0.0 21.4 %shard_map.55.o = bf16[4,64,32,128]{3,2,1,0:T(8,128)(2,1)S(1)} custom-call(bf16[4,64,32,128]{3,2,1,0:T(8,128)(2,1)} %bitcast.5, bf16[3,3,128,128]{3,2,1,0:T(8,128)(2,1)} %w_in.1, bf16[3,3,128,128]{3,2,1,0:T(8,128)(2,1)} %w_out.1, f32[4,128]{1,0:T(4,128)} %decay_in.1, f32[1,128]{1,0:T(1,128)} %bitcast.6), custom_call_target="tpu_custom_call" | custom-call | tf_op jit(solution)/shard_map/pallas_call | solution.py:437
  21.4 1.3 %shard_map.56 = bf16[4,64,32,128]{3,2,1,0:T(8,128)(2,1)} custom-call(bf16[4,64,32,128]{3,2,1,0:T(8,128)(2,1)S(1)} %shard_map.55.o), custom_call_target="tpu_custom_call" | custom-call | tf_op jit(solution)/shard_map/pallas_call | solution.py:480

commit v9 on v8

--- a/solution.py
+++ b/solution.py
@@ -104,15 +104,20 @@
         return lax.rem(me + by + tiles, tiles)
 
     first = me == 0
-    near = [both(there, jnp.logical_not(first)) for _, there in around]
-    to_first = [both(there, at(by) == 0) for by, there in around]
+    starts_line = lax.rem(me, LINE) == 0
+    far, far_for = [], []
+    for i, (by, there) in enumerate(around):
+        far.append(both(there, starts_line if i in (0, 4, 6) else first))
+        target_far = lax.rem(at(by), LINE) == 0 if i in (1, 5, 7) else at(by) == 0
+        far_for.append(both(there, target_far))
+    near = [both(there, jnp.logical_not(far[i])) for i, (_, there) in enumerate(around)]
 
     barrier = pltpu.get_barrier_semaphore()
     greeted = jnp.int32(1)
     for i, (by, there) in enumerate(around):
         greeted = greeted + near[i].astype(jnp.int32)
 
-        @pl.when(both(there, jnp.logical_not(to_first[i])))
+        @pl.when(both(there, jnp.logical_not(far_for[i])))
         def _():
             pl.semaphore_signal(barrier, inc=1, device_id=(tm, at(by)), device_id_type=MESH)
 
@@ -127,15 +132,11 @@
     for c in placed[:first_needed]:
         c.start()
 
-    def greet():
-        pl.semaphore_wait(barrier, greeted)
-        for i, (by, _) in enumerate(around):
-            @pl.when(to_first[i])
-            def _():
-                pl.semaphore_signal(far_sem.at[i], inc=1, device_id=(tm, at(by)), device_id_type=MESH)
-
-    starts_line = lax.rem(me, LINE) == 0
-    pl.when(jnp.logical_not(starts_line))(greet)
+    pl.semaphore_wait(barrier, greeted)
+    for i, (by, _) in enumerate(around):
+        @pl.when(far_for[i])
+        def _():
+            pl.semaphore_signal(far_sem.at[i], inc=1, device_id=(tm, at(by)), device_id_type=MESH)
 
     for f in range(count):
         loads[f].wait()
@@ -224,30 +225,26 @@
             lhs = pair_rows(frame_rows(f, pl.ds(2 * q, 2 * size + 2)), size)
             recur(f, q, size, mm(lhs, weights1[...]))
 
-    greet_at = jnp.where(starts_line, 1, 0)
-
-    @pl.loop(0, 2)
-    def _(step):
-        @pl.when(step == greet_at)
-        def _():
-            pl.when(starts_line)(greet)
-            for i in (1, 5, 7, 4, 6, 3):
-                pl.when(near[i])(sends[i].start)
-
-        @pl.when(step != greet_at)
-        def _():
-            for c in placed[first_needed:]:
-                c.start()
-            pair_zeros(pw1)
-            for c in placed[:first_needed]:
-                c.wait()
-            first_conv(0)
-
+    def send_far():
+        for i, opposite in ((2, 3), (3, 2), (4, 7), (5, 6), (6, 5), (7, 4), (0, 1), (1, 0)):
+            @pl.when(far[i])
+            def _():
+                pl.semaphore_wait(far_sem.at[opposite], 1)
+                sends[i].start()
+
+    for i in (1, 5, 7, 4, 6, 3, 2):
+        pl.when(near[i])(sends[i].start)
+    for c in placed[first_needed:]:
+        c.start()
+    pair_zeros(pw1)
+    for c in placed[:first_needed]:
+        c.wait()
+    first_conv(0)
     hands[0].start()
-    for i in (0, 2):
-        pl.when(near[i])(sends[i].start)
+    pl.when(near[0])(sends[0].start)
     first_conv(1)
     hands[1].start()
+    pl.when(both(starts_line, jnp.logical_not(first)))(send_far)
 
     factors = []
     for f in range(count):
@@ -302,13 +299,7 @@
     hands[1].wait_recv()
     second_conv(1, range(count // 2))
 
-    @pl.when(first)
-    def _():
-        for i, opposite in ((2, 3), (3, 2), (4, 7), (5, 6), (6, 5), (7, 4), (0, 1), (1, 0)):
-            @pl.when(around[i][1])
-            def _():
-                pl.semaphore_wait(far_sem.at[opposite], 1)
-                sends[i].start()
+    pl.when(first)(send_far)
 
     def arrive(*which):
         for i in which:

time: 22.9 us -> 20.2 us (0.88)
  Pallas kernels: 22.7 us -> 20 us
    pallas_call x1, Pallas kernels: 21.4 us -> 18.7 us  [per_device(): pl.pallas_call(functools.partial(kernel, TROWS), out_shape=pltpu.VMEM((co...]
where the time goes in v9:
time: 20.2 us; the launch traced here: 20 us
  Pallas kernels  20 us (99%)
    pallas_call x1, Pallas kernels, per_device(): pl.pallas_call(functools.partial(kernel, TROWS), out_shape=pltpu.VMEM((co...  18.7 us
    pallas_call x1, Pallas kernels, per_device(): pl.pallas_call(write_out, out_shape=jax.ShapeDtypeStruct(out.shape, BF),...  1.35 us

profile of v9, /device:TPU:1, one launch (start us, length us, event | category | flops | bytes accessed | tf_op | source)
XLA Modules:
  0.0 20.0 jit_solution(12080407576396831724)
XLA Ops:
  0.0 18.7 %shard_map.55.o = bf16[4,64,32,128]{3,2,1,0:T(8,128)(2,1)S(1)} custom-call(bf16[4,64,32,128]{3,2,1,0:T(8,128)(2,1)} %bitcast.5, bf16[3,3,128,128]{3,2,1,0:T(8,128)(2,1)} %w_in.1, bf16[3,3,128,128]{3,2,1,0:T(8,128)(2,1)} %w_out.1, f32[4,128]{1,0:T(4,128)} %decay_in.1, f32[1,128]{1,0:T(1,128)} %bitcast.6), custom_call_target="tpu_custom_call" | custom-call | tf_op jit(solution)/shard_map/pallas_call | solution.py:428
  18.7 1.3 %shard_map.56 = bf16[4,64,32,128]{3,2,1,0:T(8,128)(2,1)} custom-call(bf16[4,64,32,128]{3,2,1,0:T(8,128)(2,1)S(1)} %shard_map.55.o), custom_call_target="tpu_custom_call" | custom-call | tf_op jit(solution)/shard_map/pallas_call | solution.py:471

commit v10 on v9

--- a/solution.py
+++ b/solution.py
@@ -15,6 +15,7 @@
 MESH = pl.DeviceIdType.MESH
 
 TAPS = 3
+PIECES = 1
 
 
 def mm(lhs, rhs):
@@ -138,22 +139,15 @@
         def _():
             pl.semaphore_signal(far_sem.at[i], inc=1, device_id=(tm, at(by)), device_id_type=MESH)
 
-    for f in range(count):
-        loads[f].wait()
-        stage[0] = x[f, 2 : 2 + rows, 0:16, :].astype(F32)[:, 0:8, :].reshape(rows * 8, C)
-        stage[1] = x[f, 2 : 2 + rows, cols - 16 : cols, :].astype(F32)[:, 8:16, :].reshape(rows * 8, C)
-        for s in range(2):
-            for n in range(2):
-                offset = n if s == 0 else 7 - n
-                edge[s, n, f] = stage[s, pl.ds(offset, rows, stride=8), :].astype(BF)
-                for t in range(2):
-                    ends = pl.ds(offset + t * (rows - 2) * 8, 2, stride=8)
-                    cstage[s, t, n, 2 * f : 2 * f + 2] = stage[s, ends, :]
-    rest = jnp.zeros((8, C), F32)
-    for s in range(2):
-        for t in range(2):
-            for n in range(2):
-                corner[s, t, n] = jnp.concatenate([cstage[s, t, n], rest], axis=0).astype(BF)
+    def edges(s, f):
+        begin, keep = (0, slice(0, 8)) if s == 0 else (cols - 16, slice(8, 16))
+        stage[s] = x[f, 2 : 2 + rows, begin : begin + 16, :].astype(F32)[:, keep, :].reshape(rows * 8, C)
+        for n in range(2):
+            offset = n if s == 0 else 7 - n
+            edge[s, n, f] = stage[s, pl.ds(offset, rows, stride=8), :].astype(BF)
+            for t in range(2):
+                ends = pl.ds(offset + t * (rows - 2) * 8, 2, stride=8)
+                cstage[s, t, n, 2 * f : 2 * f + 2] = stage[s, ends, :]
 
     plan = [
         (edge.at[0], z.at[1]),
@@ -172,6 +166,18 @@
         )
         for i, (src, dst) in enumerate(plan)
     ]
+    for f in range(count):
+        loads[f].wait()
+        edges(1, f)
+    pl.when(near[1])(sends[1].start)
+    for f in range(count):
+        edges(0, f)
+    rest = jnp.zeros((8, C), F32)
+    for s in range(2):
+        for t in range(2):
+            for n in range(2):
+                corner[s, t, n] = jnp.concatenate([cstage[s, t, n], rest], axis=0).astype(BF)
+
     comes = [around[i ^ 1][1] if i < 4 else around[11 - i][1] for i in range(8)]
     in_tile = lax.broadcasted_iota(jnp.int32, (1, 8, C), 1)
 
@@ -198,7 +204,8 @@
     late_hands = [
         exchange(2, lo.at[pl.ds(0, 1)], inc.at[pl.ds(0, 1)]),
         exchange(3, lo.at[pl.ds(pairs, 1)], inc.at[pl.ds(pairs, 1)]),
-        exchange(4, so, si),
+        exchange(4, so.at[0], si.at[0]),
+        exchange(5, so.at[1], si.at[1]),
     ]
     weights1 = pw1.reshape(4 * TAPS * C, 2 * C)
     weights2 = pw2.reshape(4 * TAPS * C, 2 * C)
@@ -226,13 +233,13 @@
             recur(f, q, size, mm(lhs, weights1[...]))
 
     def send_far():
-        for i, opposite in ((2, 3), (3, 2), (4, 7), (5, 6), (6, 5), (7, 4), (0, 1), (1, 0)):
+        for i, opposite in ((0, 1), (4, 7), (6, 5), (2, 3), (3, 2), (1, 0), (5, 6), (7, 4)):
             @pl.when(far[i])
             def _():
                 pl.semaphore_wait(far_sem.at[opposite], 1)
                 sends[i].start()
 
-    for i in (1, 5, 7, 4, 6, 3, 2):
+    for i in (5, 7, 4, 6, 3, 2):
         pl.when(near[i])(sends[i].start)
     for c in placed[first_needed:]:
         c.start()
@@ -319,69 +326,45 @@
     late_hands[0].start()
     late_hands[1].start()
 
-    sides_at = jnp.where(first, 1, 0)
-
-    @pl.loop(0, 2)
-    def _(step):
-        @pl.when(step == sides_at)
-        def _():
-            for c in placed[then_needed:]:
-                c.wait()
-            arrive(0, 4, 6, 1, 5, 7)
-            for s in range(2):
-                lines = [jnp.concatenate([z[s, 0, f], z[s, 1, f], edge[s, 0, f]], axis=-1) for f in range(count)]
-                for t in range(2):
-                    mine = jnp.concatenate([rim[t, s, pl.ds(7 * s, 8, stride=8), :], rest], axis=0).astype(BF)
-                    lines.append(jnp.concatenate([zc[s, t, 0], zc[s, t, 1], mine], axis=-1))
-                lhs = jnp.concatenate(lines, axis=0)
-                for a in range(3):
-                    result = mm(lhs, sw1[s, a].reshape(3 * C, 2 * C))
-                    for e in range(2):
-                        part = result[:, e * C : (e + 1) * C]
-                        for f in range(count):
-                            base = 2 * (8 + f * tall)
-                            y[s, a, e, pl.ds(base + 16, rows, stride=2), :] = part[f * rows : (f + 1) * rows]
-                            for t in range(2):
-                                begin = count * rows + 16 * t + 2 * f
-                                y[s, a, e, pl.ds(base + 12 + t * 2 * (rows + 2), 2, stride=2), :] = part[begin : begin + 2]
-
-            for s in range(2):
-                inside = jnp.where(left if s == 0 else right, 1.0, 0.0).astype(F32)
-                for e in range(2):
-                    state = None
-                    for f in range(count):
-                        base = 2 * (8 + f * tall)
-                        drive = sum(y[s, a, e, pl.ds(base + 2 * (a - 1), tall, stride=2), :] for a in range(3))
-                        if e == 0:
-                            drive = drive * inside
-                        state = drive if f == 0 else decay[f : f + 1, :] * state + drive
-                        whole = state
-                        if e == 1:
-                            whole = state + loc[f, pl.ds(s * (cols - 1), tall, stride=cols), :]
-                        ss[s, e, f] = whole
-                    so[s, e] = whole.astype(BF)
-            late_hands[2].start()
-
-        @pl.when(step != sides_at)
-        def _():
-            second_conv(1, range(count // 2, count))
-            late_hands[0].wait_recv()
-            late_hands[1].wait_recv()
+    def side_in(s):
+        arrive(*((1, 5, 7) if s == 0 else (0, 4, 6)))
+        lines = [jnp.concatenate([z[s, 0, f], z[s, 1, f], edge[s, 0, f]], axis=-1) for f in range(count)]
+        for t in range(2):
+            mine = jnp.concatenate([rim[t, s, pl.ds(7 * s, 8, stride=8), :], rest], axis=0).astype(BF)
+            lines.append(jnp.concatenate([zc[s, t, 0], zc[s, t, 1], mine], axis=-1))
+        lhs = jnp.concatenate(lines, axis=0)
+        for a in range(3):
+            result = mm(lhs, sw1[s, a].reshape(3 * C, 2 * C))
+            for e in range(2):
+                part = result[:, e * C : (e + 1) * C]
+                for f in range(count):
+                    base = 2 * (8 + f * tall)
+                    y[s, a, e, pl.ds(base + 16, rows, stride=2), :] = part[f * rows : (f + 1) * rows]
+                    for t in range(2):
+                        begin = count * rows + 16 * t + 2 * f
+                        y[s, a, e, pl.ds(base + 12 + t * 2 * (rows + 2), 2, stride=2), :] = part[begin : begin + 2]
+        inside = jnp.where(left if s == 0 else right, 1.0, 0.0).astype(F32)
+        for e in range(2):
+            state = None
             for f in range(count):
-                settle(f, 0, (up, None))
-                settle(f, pairs, (None, down))
-            lhs = [pair_rows([s3[f, 2 * p : 2 * p + 4]], 1) for p in (0, pairs - 1) for f in range(count)]
-            result = mm_halves(jnp.concatenate(lhs, axis=0), weights2[...])
-            for n, p in enumerate((0, pairs - 1)):
-                for f in range(count):
-                    finish(f, p, 1, result[(n * count + f) * cols : (n * count + f + 1) * cols])
-
-    late_hands[2].wait_recv()
-    place = lax.broadcasted_iota(jnp.int32, (tall, C), 0)
-    off = jnp.logical_or(
-        both(place == 7, jnp.logical_not(up)), both(place == rows + 8, jnp.logical_not(down))
-    )
-    for s in range(2):
+                base = 2 * (8 + f * tall)
+                drive = sum(y[s, a, e, pl.ds(base + 2 * (a - 1), tall, stride=2), :] for a in range(3))
+                if e == 0:
+                    drive = drive * inside
+                state = drive if f == 0 else decay[f : f + 1, :] * state + drive
+                whole = state
+                if e == 1:
+                    whole = state + loc[f, pl.ds(s * (cols - 1), tall, stride=cols), :]
+                ss[s, e, f] = whole
+            so[s, e] = whole.astype(BF)
+        late_hands[2 + s].start()
+
+    def side_out(s):
+        late_hands[2 + s].wait_recv()
+        place = lax.broadcasted_iota(jnp.int32, (tall, C), 0)
+        off = jnp.logical_or(
+            both(place == 7, jnp.logical_not(up)), both(place == rows + 8, jnp.logical_not(down))
+        )
         sides = []
         for f in range(count):
             pair = [
@@ -393,16 +376,42 @@
             result = mm(lhs, sw2[s, a].reshape(2 * C, 2 * C))
             for e in range(2):
                 y2[s, a, e, pl.ds(16, count * tall, stride=2), :] = result[:, e * C : (e + 1) * C]
-
-    for f in range(count):
-        base = 2 * (8 + f * tall + 8)
-        for s in range(2):
+        begin = s * (cols - 8)
+        for f in range(count):
+            base = 2 * (8 + f * tall + 8)
             for e in range(2):
                 here = pl.ds(e if s == 0 else 7 - e, rows, stride=8)
                 fix = sum(y2[s, a, e, pl.ds(base + 2 * (a - 1), rows, stride=2), :] for a in range(3))
                 ot[s, f, here, :] = ot[s, f, here, :] + fix
-        o[f, :, 0:8] = ot[0, f].reshape(rows, 8, C).astype(BF)
-        o[f, :, cols - 8 :] = ot[1, f].reshape(rows, 8, C).astype(BF)
+            o[f, :, begin : begin + 8] = ot[s, f].reshape(rows, 8, C).astype(BF)
+
+    for c in placed[then_needed:]:
+        c.wait()
+    ends_line = lax.rem(me, LINE) == LINE - 1
+    orders = ((ends_line, 0, 1), (jnp.logical_not(ends_line), 1, 0))
+    for here, early, last in orders:
+        @pl.when(here)
+        def _():
+            side_in(early)
+
+    second_conv(1, range(count // 2, count))
+    late_hands[0].wait_recv()
+    late_hands[1].wait_recv()
+    for f in range(count):
+        settle(f, 0, (up, None))
+        settle(f, pairs, (None, down))
+    lhs = [pair_rows([s3[f, 2 * p : 2 * p + 4]], 1) for p in (0, pairs - 1) for f in range(count)]
+    result = mm_halves(jnp.concatenate(lhs, axis=0), weights2[...])
+    for n, p in enumerate((0, pairs - 1)):
+        for f in range(count):
+            finish(f, p, 1, result[(n * count + f) * cols : (n * count + f + 1) * cols])
+
+    for here, early, last in orders:
+        @pl.when(here)
+        def _():
+            side_in(last)
+            side_out(early)
+            side_out(last)
 
     for i, c in enumerate(sends):
         pl.when(around[i][1])(c.wait_send)
@@ -411,7 +420,14 @@
 
 
 def write_out(o, out, sem):
-    stores = [pltpu.make_async_copy(o.at[f], out.at[f], sem.at[f]) for f in range(o.shape[0])]
+    size = o.shape[1] // PIECES
+    stores = [
+        pltpu.make_async_copy(
+            o.at[f, pl.ds(n * size, size)], out.at[f, pl.ds(n * size, size)], sem.at[f, n]
+        )
+        for f in range(o.shape[0])
+        for n in range(PIECES)
+    ]
     for c in stores:
         c.start()
     for c in stores:
@@ -460,8 +476,8 @@
             pltpu.SemaphoreType.DMA((28,)),
             pltpu.SemaphoreType.DMA((8,)),
             pltpu.SemaphoreType.DMA((8,)),
-            pltpu.SemaphoreType.DMA((5,)),
-            pltpu.SemaphoreType.DMA((5,)),
+            pltpu.SemaphoreType.DMA((6,)),
+            pltpu.SemaphoreType.DMA((6,)),
             pltpu.SemaphoreType.REGULAR((8,)),
         ],
         compiler_params=pltpu.CompilerParams(
@@ -473,7 +489,7 @@
         out_shape=jax.ShapeDtypeStruct(out.shape, BF),
         in_specs=[vmem],
         out_specs=hbm,
-        scratch_shapes=[pltpu.SemaphoreType.DMA((count,))],
+        scratch_shapes=[pltpu.SemaphoreType.DMA((count, PIECES))],
         compiler_params=pltpu.CompilerParams(vmem_limit_bytes=2**20),
     )(pltpu.with_memory_space_constraint(out, pltpu.VMEM))
     return out.reshape(count, 1, rows, cols, C)

time: 20.2 us -> 19.5 us (0.965)
  Pallas kernels: 20 us -> 19.4 us
    pallas_call x1, Pallas kernels: 18.7 us -> 18 us  [per_device(): pl.pallas_call(functools.partial(kernel, TROWS), out_shape=pltpu.VMEM((co...]
where the time goes in v10:
time: 19.5 us; the launch traced here: 19.4 us
  Pallas kernels  19.4 us (99%)
    pallas_call x1, Pallas kernels, per_device(): pl.pallas_call(functools.partial(kernel, TROWS), out_shape=pltpu.VMEM((co...  18 us
    pallas_call x1, Pallas kernels, per_device(): pl.pallas_call(write_out, out_shape=jax.ShapeDtypeStruct(out.shape, BF),...  1.35 us

profile of v10, /device:TPU:1, one launch (start us, length us, event | category | flops | bytes accessed | tf_op | source)
XLA Modules:
  0.0 19.4 jit_solution(8573152779623966334)
XLA Ops:
  0.0 18.0 %shard_map.55.o = bf16[4,64,32,128]{3,2,1,0:T(8,128)(2,1)S(1)} custom-call(bf16[4,64,32,128]{3,2,1,0:T(8,128)(2,1)} %bitcast.5, bf16[3,3,128,128]{3,2,1,0:T(8,128)(2,1)} %w_in.1, bf16[3,3,128,128]{3,2,1,0:T(8,128)(2,1)} %w_out.1, f32[4,128]{1,0:T(4,128)} %decay_in.1, f32[1,128]{1,0:T(1,128)} %bitcast.6), custom_call_target="tpu_custom_call" | custom-call | tf_op jit(solution)/shard_map/pallas_call | solution.py:444
  18.0 1.3 %shard_map.56 = bf16[4,64,32,128]{3,2,1,0:T(8,128)(2,1)} custom-call(bf16[4,64,32,128]{3,2,1,0:T(8,128)(2,1)S(1)} %shard_map.55.o), custom_call_target="tpu_custom_call" | custom-call | tf_op jit(solution)/shard_map/pallas_call | solution.py:487

commit v11 on v10

--- a/solution.py
+++ b/solution.py
@@ -232,8 +232,8 @@
             lhs = pair_rows(frame_rows(f, pl.ds(2 * q, 2 * size + 2)), size)
             recur(f, q, size, mm(lhs, weights1[...]))
 
-    def send_far():
-        for i, opposite in ((0, 1), (4, 7), (6, 5), (2, 3), (3, 2), (1, 0), (5, 6), (7, 4)):
+    def send_far(*which):
+        for i, opposite in which:
             @pl.when(far[i])
             def _():
                 pl.semaphore_wait(far_sem.at[opposite], 1)
@@ -251,7 +251,8 @@
     pl.when(near[0])(sends[0].start)
     first_conv(1)
     hands[1].start()
-    pl.when(both(starts_line, jnp.logical_not(first)))(send_far)
+    to_left, to_rest = ((0, 1), (4, 7), (6, 5)), ((2, 3), (3, 2), (1, 0), (5, 6), (7, 4))
+    pl.when(both(starts_line, jnp.logical_not(first)))(functools.partial(send_far, *to_left))
 
     factors = []
     for f in range(count):
@@ -306,7 +307,7 @@
     hands[1].wait_recv()
     second_conv(1, range(count // 2))
 
-    pl.when(first)(send_far)
+    pl.when(first)(functools.partial(send_far, *to_rest))
 
     def arrive(*which):
         for i in which:
@@ -325,6 +326,7 @@
             recur(f, q, 1, drive[(n * count + f) * cols : (n * count + f + 1) * cols])
     late_hands[0].start()
     late_hands[1].start()
+    pl.when(first)(functools.partial(send_far, *to_left))
 
     def side_in(s):
         arrive(*((1, 5, 7) if s == 0 else (0, 4, 6)))

time: 19.5 us -> 19.5 us (level)
  no operation moved by 1% of the time
where the time goes in v11:
time: 19.5 us; the launch traced here: 19.4 us
  Pallas kernels  19.4 us (99%)
    pallas_call x1, Pallas kernels, per_device(): pl.pallas_call(functools.partial(kernel, TROWS), out_shape=pltpu.VMEM((co...  18 us
    pallas_call x1, Pallas kernels, per_device(): pl.pallas_call(write_out, out_shape=jax.ShapeDtypeStruct(out.shape, BF),...  1.35 us

profile of v11, /device:TPU:1, one launch (start us, length us, event | category | flops | bytes accessed | tf_op | source)
XLA Modules:
  0.0 19.4 jit_solution(7005735590600342930)
XLA Ops:
  0.0 18.0 %shard_map.55.o = bf16[4,64,32,128]{3,2,1,0:T(8,128)(2,1)S(1)} custom-call(bf16[4,64,32,128]{3,2,1,0:T(8,128)(2,1)} %bitcast.5, bf16[3,3,128,128]{3,2,1,0:T(8,128)(2,1)} %w_in.1, bf16[3,3,128,128]{3,2,1,0:T(8,128)(2,1)} %w_out.1, f32[4,128]{1,0:T(4,128)} %decay_in.1, f32[1,128]{1,0:T(1,128)} %bitcast.6), custom_call_target="tpu_custom_call" | custom-call | tf_op jit(solution)/shard_map/pallas_call | solution.py:446
  18.0 1.3 %shard_map.56 = bf16[4,64,32,128]{3,2,1,0:T(8,128)(2,1)} custom-call(bf16[4,64,32,128]{3,2,1,0:T(8,128)(2,1)S(1)} %shard_map.55.o), custom_call_target="tpu_custom_call" | custom-call | tf_op jit(solution)/shard_map/pallas_call | solution.py:489

commit v12 on v11

--- a/solution.py
+++ b/solution.py
@@ -72,7 +72,7 @@
 def kernel(
     trows, frames, w_in, w_out, decay_in, skip_in, o,
     x, x3, s3, loc, pw1, pw2, sw1, sw2, edge, corner, z, zc, y, y2, ss, stage, cstage, rim, lo, inc, so, si, ot, decay, skip,
-    load_sem, w_sem, send_sem, recv_sem, tsend_sem, trecv_sem, far_sem,
+    load_sem, w_sem, send_sem, recv_sem, tsend_sem, trecv_sem, far_sem, right_send, right_recv,
 ):
     count, rows, cols, _ = frames.shape
     tiles = lax.axis_size("tile")
@@ -166,10 +166,18 @@
         )
         for i, (src, dst) in enumerate(plan)
     ]
+    rights = [
+        pltpu.make_async_remote_copy(
+            src_ref=edge.at[1, :, f], dst_ref=z.at[0, :, f], send_sem=right_send.at[f], recv_sem=right_recv.at[f],
+            device_id=(tm, at(1)), device_id_type=MESH,
+        )
+        for f in range(count)
+    ]
+
     for f in range(count):
         loads[f].wait()
         edges(1, f)
-    pl.when(near[1])(sends[1].start)
+        pl.when(near[1])(rights[f].start)
     for f in range(count):
         edges(0, f)
     rest = jnp.zeros((8, C), F32)
@@ -237,7 +245,8 @@
             @pl.when(far[i])
             def _():
                 pl.semaphore_wait(far_sem.at[opposite], 1)
-                sends[i].start()
+                for c in rights if i == 1 else [sends[i]]:
+                    c.start()
 
     for i in (5, 7, 4, 6, 3, 2):
         pl.when(near[i])(sends[i].start)
@@ -311,7 +320,8 @@
 
     def arrive(*which):
         for i in which:
-            pl.when(comes[i])(sends[i].wait_recv)
+            for c in rights if i == 1 else [sends[i]]:
+                pl.when(comes[i])(c.wait_recv)
 
     arrive(2, 3)
     for f in range(count):
@@ -415,8 +425,9 @@
             side_out(early)
             side_out(last)
 
-    for i, c in enumerate(sends):
-        pl.when(around[i][1])(c.wait_send)
+    for i, (_, there) in enumerate(around):
+        for c in rights if i == 1 else [sends[i]]:
+            pl.when(there)(c.wait_send)
     for c in hands + late_hands:
         c.wait_send()
 
@@ -481,6 +492,8 @@
             pltpu.SemaphoreType.DMA((6,)),
             pltpu.SemaphoreType.DMA((6,)),
             pltpu.SemaphoreType.REGULAR((8,)),
+            pltpu.SemaphoreType.DMA((count,)),
+            pltpu.SemaphoreType.DMA((count,)),
         ],
         compiler_params=pltpu.CompilerParams(
             collective_id=0, has_side_effects=True, vmem_limit_bytes=48 * 2**20

time: 19.5 us -> 19.5 us (level)
  no operation moved by 1% of the time
where the time goes in v12:
time: 19.5 us; the launch traced here: 19.4 us
  Pallas kernels  19.4 us (99%)
    pallas_call x1, Pallas kernels, per_device(): pl.pallas_call(functools.partial(kernel, TROWS), out_shape=pltpu.VMEM((co...  18 us
    pallas_call x1, Pallas kernels, per_device(): pl.pallas_call(write_out, out_shape=jax.ShapeDtypeStruct(out.shape, BF),...  1.35 us

profile of v12, /device:TPU:1, one launch (start us, length us, event | category | flops | bytes accessed | tf_op | source)
XLA Modules:
  0.0 19.4 jit_solution(5423328104769246752)
XLA Ops:
  0.0 18.0 %shard_map.55.o = bf16[4,64,32,128]{3,2,1,0:T(8,128)(2,1)S(1)} custom-call(bf16[4,64,32,128]{3,2,1,0:T(8,128)(2,1)} %bitcast.5, bf16[3,3,128,128]{3,2,1,0:T(8,128)(2,1)} %w_in.1, bf16[3,3,128,128]{3,2,1,0:T(8,128)(2,1)} %w_out.1, f32[4,128]{1,0:T(4,128)} %decay_in.1, f32[1,128]{1,0:T(1,128)} %bitcast.6), custom_call_target="tpu_custom_call" | custom-call | tf_op jit(solution)/shard_map/pallas_call | solution.py:457
  18.0 1.3 %shard_map.56 = bf16[4,64,32,128]{3,2,1,0:T(8,128)(2,1)} custom-call(bf16[4,64,32,128]{3,2,1,0:T(8,128)(2,1)S(1)} %shard_map.55.o), custom_call_target="tpu_custom_call" | custom-call | tf_op jit(solution)/shard_map/pallas_call | solution.py:502
